TPU v7x, 512 devices: a whole 4x8x8 slice. The times are simulated.
512 devices in a mesh: expert: 64 (over z, y), dp: 8 (over x, core).
Axes of the slice: x: 4, y: 8, z: 8, core: 2. Of those that a mesh axis runs over, the one named last changes fastest.
Arguments:
- tokens: bfloat16 [8192, 4096], P('expert', 'dp'), may hold values from -6 to 6
- route_ids: int32 [8192, 8], P('expert'), may hold values from 0 to 63, as said below
- route_gates: float32 [8192, 8], P('expert'), may hold values from 0.05 to 0.5
- keep_mask: int32 [8192, 8], P('expert'), may hold values from 0 to 1, as said below
- old_gate: bfloat16 [64, 4096, 768], P('expert', 'dp'), may hold values from -0.09375 to 0.09375
- old_up: bfloat16 [64, 4096, 768], P('expert', 'dp'), may hold values from -0.09375 to 0.09375
- old_down: bfloat16 [64, 768, 4096], P('expert', None, 'dp'), may hold values from -0.21875 to 0.21875
- placement_map: int32 [64], replicated, may hold values from 0 to 63, each once
Outputs:
- mixed: bfloat16 [8192, 4096], P('expert', 'dp')
- new_gate: bfloat16 [64, 4096, 768], P('expert', 'dp')
- new_up: bfloat16 [64, 4096, 768], P('expert', 'dp')
- new_down: bfloat16 [64, 768, 4096], P('expert', None, 'dp')
Inputs may be any that keep to these rules, and one draw needn't show every extreme that they name: `route_ids`: each token's 8 slots are distinct. `keep_mask`: in each token group of 128 tokens at most 16 kept assignments name any one slot, and in every group some slot has exactly 16; dropped assignments are those past the first 16 of their slot in the group's order of tokens and k.
All inputs are finite; a program needn't handle non-finite values.
Results may differ from a plain program's by a relative error of at most 0.015.
Values may be sent and summed in bfloat16 or wider, within the bound.
No kernel may reach another device: no remote copies, remote signals or barrier semaphores. Data moves between devices by JAX's collectives and lax.ppermute only.
A program may use at most 64 MiB of HBM per device.

v0:
```python
import jax
import jax.numpy as jnp
from jax import lax
from jax.sharding import PartitionSpec as P

CAP = 16


def shortened(shard):

    def short(part):
        return part.astype(jnp.bfloat16) if part.dtype == jnp.float32 else part

    return jax.tree.map(short, shard)


def shards(tokens, route_ids, route_gates, keep_mask, old_gate, old_up, old_down, placement_map):
    replicas = lax.axis_size("expert")
    group_rows = tokens.shape[0]
    width_share = tokens.shape[1]
    top_count = route_ids.shape[1]
    hidden_size = old_gate.shape[2]
    gate_local = old_gate[0]
    up_local = old_up[0]
    down_local = old_down[0]
    columns = jnp.arange(replicas, dtype=jnp.int32)
    matching = (placement_map[None, :] == columns[:, None]).astype(jnp.bfloat16)
    outgoing_parts = (
        gate_local.reshape(replicas, -1, hidden_size),
        up_local.reshape(replicas, -1, hidden_size),
        down_local.reshape(replicas, -1, width_share),
    )
    spread = (
        lax.all_to_all(outgoing_parts[0], "expert", split_axis=0, concat_axis=0, tiled=True),
        lax.all_to_all(outgoing_parts[1], "expert", split_axis=0, concat_axis=0, tiled=True),
        lax.all_to_all(outgoing_parts[2], "expert", split_axis=0, concat_axis=0, tiled=True),
    )
    ordered = tuple(
        (
            jnp.einsum(
                "so,oab->sab", matching, block_part, preferred_element_type=jnp.float32
            ).astype(jnp.bfloat16)
            for block_part in spread
        )
    )
    collected = jax.tree.map(
        lambda part, own: part.astype(own.dtype),
        lax.all_to_all(shortened(ordered), "expert", split_axis=0, concat_axis=0, tiled=True),
        ordered,
    )
    gate_moved = collected[0].reshape(gate_local.shape)
    up_moved = collected[1].reshape(up_local.shape)
    down_moved = collected[2].reshape(down_local.shape)
    flat_target = route_ids.reshape(-1)
    flat_kept = keep_mask.reshape(-1)
    onehot = (flat_target[:, None] == columns[None, :]).astype(jnp.int32) * flat_kept[:, None]
    before = jnp.cumsum(onehot, axis=0) - onehot
    ranking = jnp.sum(before * onehot, axis=1)
    slot_index = jnp.where(flat_kept > 0, flat_target * CAP + ranking, -1).reshape(
        group_rows, top_count
    )
    slot_range = jnp.arange(replicas * CAP, dtype=jnp.int32)
    slot_hits = slot_index[:, :, None] == slot_range[None, None, :]
    dispatch_mat = jnp.any(slot_hits, axis=1).astype(jnp.bfloat16)
    combine_mat = jnp.sum(jnp.where(slot_hits, route_gates[:, :, None], 0.0), axis=1)
    outgoing = lax.dot_general(
        dispatch_mat, tokens, (((0,), (0,)), ((), ())), preferred_element_type=jnp.float32
    )
    outgoing = outgoing.astype(jnp.bfloat16).reshape(replicas, CAP, width_share)
    received = lax.all_to_all(outgoing, "expert", split_axis=0, concat_axis=0, tiled=True)
    slot_count = received.shape[1]
    arrived = received.reshape(-1, width_share)
    gate_part = jnp.dot(arrived, gate_moved, preferred_element_type=jnp.float32)
    up_part = jnp.dot(arrived, up_moved, preferred_element_type=jnp.float32)
    gate_sum = lax.psum(gate_part.astype(jnp.bfloat16), "dp").astype(jnp.float32)
    up_sum = lax.psum(up_part.astype(jnp.bfloat16), "dp").astype(jnp.float32)
    hidden = (jax.nn.silu(gate_sum) * up_sum).astype(jnp.bfloat16)
    produced = jnp.dot(hidden, down_moved, preferred_element_type=jnp.float32).astype(jnp.bfloat16)
    produced = produced.reshape(replicas, slot_count, width_share)
    returned = lax.all_to_all(produced, "expert", split_axis=0, concat_axis=0, tiled=True)
    combined = jnp.dot(
        combine_mat,
        returned.reshape(-1, width_share).astype(jnp.float32),
        precision=lax.Precision.HIGHEST,
    )
    mixed = (tokens.astype(jnp.float32) + combined).astype(jnp.bfloat16)
    return (mixed, gate_moved[None], up_moved[None], down_moved[None])


def solution(mesh):
    in_specs = (
        P("expert", "dp"),
        P("expert", None),
        P("expert", None),
        P("expert", None),
        P("expert", "dp", None),
        P("expert", "dp", None),
        P("expert", None, "dp"),
        P(),
    )
    out_specs = (
        P("expert", "dp"),
        P("expert", "dp", None),
        P("expert", "dp", None),
        P("expert", None, "dp"),
    )
    return jax.shard_map(shards, mesh=mesh, in_specs=in_specs, out_specs=out_specs, check_vma=False)
```

profile of v0, /device:TPU:7, one launch (start us, length us, event | category | flops | bytes accessed | tf_op | source)
XLA Modules:
  0.0 323.8 jit_solution(11649749096678517574)
XLA Ops:
  7.2 38.2 %all_to_all.40 = bf16[64,8,768]{2,1,0:T(8,128)(2,1)S(1)} all-to-all(bf16[64,8,768]{2,1,0:T(8,128)(2,1)} %bitcast.43), channel_id=1, replica_groups=mesh['expert'=64,'dp'=8] {'expert'}, dimensions={0} | all-to-all | bytes 1572864 | tf_op jit(solution)/shard_map/all_to_all | solution.py:35
  45.4 7.6 %all-to-all-start.1 = ((bf16[64,8,768]{2,1,0:T(8,128)(2,1)}), bf16[64,8,768]{2,1,0:T(8,128)(2,1)S(1)}, u32[]{:S(2)}, u32[]{:S(2)}) async-start(bf16[64,8,768]{2,1,0:T(8,128)(2,1)} %bitcast.5), calls=%async_computation.1 | async-start | bytes 1572864 | tf_op jit(solution)/shard_map/all_to_all | solution.py:34
  53.0 0.1 copy.68
  53.1 0.1 eq.51
  53.2 0.1 eq.55
  53.3 0.1 copy.69
  53.4 0.1 mul.36
  53.5 0.1 mul.39
  53.6 18.0 %reduce-window.6 = s32[64,8,128]{2,1,0:T(8,128)S(1)} reduce-window(s32[64,8,128]{2,1,0:T(8,128)S(1)} %fusion.18, s32[]{:T(128)} %constant.6.clone.1), window={size=1x1x128 pad=0_0x0_0x127_0}, to_apply=%region_0.0 | reduce-window | flops 8323072 | bytes 524292 | tf_op jit(solution)/shard_map/reduce-window
  71.7 0.1 slice.8
  71.8 0.1 copy.70
  72.0 0.1 copy.71
  72.1 0.1 broadcast_add_fusion
  72.2 0.1 fusion.17
  72.3 0.1 reduce_sum.21
  72.4 0.1 copy.75
  72.5 1.3 fusion
  73.9 1.5 convolution_convert_fusion.2
  75.4 12.1 %all-to-all-start = ((bf16[64,16,512]{2,1,0:T(8,128)(2,1)}), bf16[64,16,512]{2,1,0:T(8,128)(2,1)S(1)}, u32[]{:S(2)}, u32[]{:S(2)}) async-start(bf16[64,16,512]{2,1,0:T(8,128)(2,1)} %bitcast.2), calls=%async_computation | async-start | bytes 2097152 | tf_op jit(solution)/shard_map/all_to_all | solution.py:70
  87.5 0.4 convolution_convert_fusion.4
  87.9 1.3 copy.80
  89.2 24.1 %all-to-all-done = bf16[64,16,512]{2,1,0:T(8,128)(2,1)S(1)} async-done(((bf16[64,16,512]{2,1,0:T(8,128)(2,1)}), bf16[64,16,512]{2,1,0:T(8,128)(2,1)S(1)}, u32[]{:S(2)}, u32[]{:S(2)}) %all-to-all-start) | async-done | bytes 1048608 | tf_op jit(solution)/shard_map/all_to_all | solution.py:70
  113.3 8.2 %all-to-all-start.4 = ((bf16[64,8,768]{2,1,0:T(8,128)(2,1)}), bf16[64,8,768]{2,1,0:T(8,128)(2,1)S(1)}, u32[]{:S(2)}, u32[]{:S(2)}) async-start(bf16[64,8,768]{2,1,0:T(8,128)(2,1)} %copy.80), calls=%async_computation.4 | async-start | bytes 1572864 | tf_op jit(solution)/shard_map/all_to_all | solution.py:48
  121.5 0.4 convolution_convert_fusion.5
  121.9 1.3 copy.78
  123.2 18.0 %all-to-all-done.4 = bf16[64,8,768]{2,1,0:T(8,128)(2,1)S(1)} async-done(((bf16[64,8,768]{2,1,0:T(8,128)(2,1)}), bf16[64,8,768]{2,1,0:T(8,128)(2,1)S(1)}, u32[]{:S(2)}, u32[]{:S(2)}) %all-to-all-start.4) | async-done | bytes 786464 | tf_op jit(solution)/shard_map/all_to_all | solution.py:48
  141.3 8.3 %all-to-all-start.2 = ((bf16[64,8,768]{2,1,0:T(8,128)(2,1)}), bf16[64,8,768]{2,1,0:T(8,128)(2,1)S(1)}, u32[]{:S(2)}, u32[]{:S(2)}) async-start(bf16[64,8,768]{2,1,0:T(8,128)(2,1)} %copy.78), calls=%async_computation.2 | async-start | bytes 1572864 | tf_op jit(solution)/shard_map/all_to_all | solution.py:48
  149.6 1.2 reshape_squeeze.11
  150.7 18.2 %all-to-all-done.2 = bf16[64,8,768]{2,1,0:T(8,128)(2,1)S(1)} async-done(((bf16[64,8,768]{2,1,0:T(8,128)(2,1)}), bf16[64,8,768]{2,1,0:T(8,128)(2,1)S(1)}, u32[]{:S(2)}, u32[]{:S(2)}) %all-to-all-start.2) | async-done | bytes 786464 | tf_op jit(solution)/shard_map/all_to_all | solution.py:48
  169.0 8.6 %all-to-all-start.5 = ((bf16[64,12,512]{2,1,0:T(8,128)(2,1)}), bf16[64,12,512]{2,1,0:T(8,128)(2,1)S(1)}, u32[]{:S(2)}, u32[]{:S(2)}) async-start(bf16[64,12,512]{2,1,0:T(8,128)(2,1)} %reshape_squeeze.11), calls=%async_computation.5 | async-start | bytes 2097152 | tf_op jit(solution)/shard_map/all_to_all | solution.py:36
  177.5 0.2 all-reduce.3.cloned.1.call-start
  177.8 3.5 %convolution_convert_fusion = bf16[1024,768]{1,0:T(8,128)(2,1)} fusion(bf16[1024,512]{1,0:T(8,128)(2,1)} %bitcast.39, bf16[64,8,768]{2,1,0:T(8,128)(2,1)S(1)} %all-to-all-done.4), kind=kOutput, calls=%fused_computation.10 | convolution fusion | flops 806092800 | bytes 3407872 | tf_op jit(solution)/shard_map/dot_general | solution.py:74
  181.2 2.1 convolution_convert_fusion.1
  183.4 19.0 %all-to-all-done.5 = bf16[64,12,512]{2,1,0:T(8,128)(2,1)S(1)} async-done(((bf16[64,12,512]{2,1,0:T(8,128)(2,1)}), bf16[64,12,512]{2,1,0:T(8,128)(2,1)S(1)}, u32[]{:S(2)}, u32[]{:S(2)}) %all-to-all-start.5) | async-done | bytes 786464 | tf_op jit(solution)/shard_map/all_to_all | solution.py:36
  202.4 1.1 convolution_convert_fusion.3
  203.5 0.4 copy.82
  203.9 33.6 %all_to_all.41 = bf16[64,12,512]{2,1,0:T(8,128)(2,1)S(1)} all-to-all(bf16[64,12,512]{2,1,0:T(8,128)(2,1)S(1)} %copy.82), channel_id=1, replica_groups=mesh['expert'=64,'dp'=8] {'expert'}, dimensions={0} | all-to-all | bytes 1572864 | tf_op jit(solution)/shard_map/all_to_all | solution.py:48
  237.5 0.2 reshape.71
  237.7 29.0 %all-reduce.3.cloned.1.call-done = (bf16[1024,768]{1,0:T(8,128)(2,1)}, bf16[1024,768]{1,0:T(8,128)(2,1)}) async-done(((bf16[1024,768]{1,0:T(8,128)(2,1)}, bf16[1024,768]{1,0:T(8,128)(2,1)}), (bf16[1024,768]{1,0:T(8,128)(2,1)}, bf16[1024,768]{1,0:T(8,128)(2,1)})) %all-reduce.3.cloned.1.call-update) | async-done | bytes 3145744 | tf_op jit(solution)/shard_map/psum | solution.py:76
  266.7 3.9 %fusion.8 = bf16[1024,512]{1,0:T(8,128)(2,1)} fusion(bf16[768,512]{1,0:T(8,128)(2,1)S(1)} %reshape.71, bf16[1024,768]{1,0:T(8,128)(2,1)} %get-tuple-element.4, bf16[1024,768]{1,0:T(8,128)(2,1)} %get-tuple-element.5), kind=kOutput, calls=%fused_computation.13 | convolution fusion | flops 812122112 | bytes 4980736 | tf_op jit(solution)/shard_map/dot_general | solution.py:78
  270.6 13.1 %all-to-all-start.7 = ((bf16[64,16,512]{2,1,0:T(8,128)(2,1)}), bf16[64,16,512]{2,1,0:T(8,128)(2,1)S(1)}, u32[]{:S(2)}, u32[]{:S(2)}) async-start(bf16[64,16,512]{2,1,0:T(8,128)(2,1)} %bitcast.41), calls=%async_computation.7 | async-start | bytes 2097152 | tf_op jit(solution)/shard_map/all_to_all | solution.py:80
  283.8 0.1 copy.76
  283.9 1.3 select_reduce_fusion
  285.2 1.1 broadcast_in_dim_reshape.14
  286.3 26.8 %all-to-all-done.7 = bf16[64,16,512]{2,1,0:T(8,128)(2,1)S(1)} async-done(((bf16[64,16,512]{2,1,0:T(8,128)(2,1)}), bf16[64,16,512]{2,1,0:T(8,128)(2,1)S(1)}, u32[]{:S(2)}, u32[]{:S(2)}) %all-to-all-start.7) | async-done | bytes 1048608 | tf_op jit(solution)/shard_map/all_to_all | solution.py:80
  313.1 2.2 fusion.11
  315.2 0.9 copy.95
  316.1 0.9 copy.96
  (27 shorter events, 0.2 us)
Async XLA Ops:
  7.2 45.9 %copy-start.7 = (s32[128,8]{0,1:T(8,128)S(1)}, s32[128,8]{0,1:T(8,128)}, u32[]{:S(2)}) copy-start(s32[128,8]{0,1:T(8,128)} %param.9) | copy-start | bytes 12292
  7.2 46.1 %copy-start.6 = (s32[128,8]{0,1:T(8,128)S(1)}, s32[128,8]{0,1:T(8,128)}, u32[]{:S(2)}) copy-start(s32[128,8]{0,1:T(8,128)} %param.11) | copy-start | bytes 12292
  45.4 30.0 %all-to-all-start.1 = ((bf16[64,8,768]{2,1,0:T(8,128)(2,1)}), bf16[64,8,768]{2,1,0:T(8,128)(2,1)S(1)}, u32[]{:S(2)}, u32[]{:S(2)}) async-start(bf16[64,8,768]{2,1,0:T(8,128)(2,1)} %bitcast.5), calls=%async_computation.1 | async-start | bytes 1572864 | tf_op jit(solution)/shard_map/all_to_all | solution.py:34
  53.2 20.7 %copy-start.5 = (bf16[128,512]{1,0:T(8,128)(2,1)S(1)}, bf16[128,512]{1,0:T(8,128)(2,1)}, u32[]{:S(2)}) copy-start(bf16[128,512]{1,0:T(8,128)(2,1)} %param.8) | copy-start | bytes 393220
  73.9 13.6 %copy-start.8 = (s32[64]{0:T(128)S(1)}, s32[64]{0:T(128)}, u32[]{:S(2)}) copy-start(s32[64]{0:T(128)} %param.15) | copy-start | bytes 772
  75.4 37.9 %all-to-all-start = ((bf16[64,16,512]{2,1,0:T(8,128)(2,1)}), bf16[64,16,512]{2,1,0:T(8,128)(2,1)S(1)}, u32[]{:S(2)}, u32[]{:S(2)}) async-start(bf16[64,16,512]{2,1,0:T(8,128)(2,1)} %bitcast.2), calls=%async_computation | async-start | bytes 2097152 | tf_op jit(solution)/shard_map/all_to_all | solution.py:70
  113.3 28.0 %copy-start.2 = (bf16[64,16,512]{2,1,0:T(8,128)(2,1)}, bf16[64,16,512]{2,1,0:T(8,128)(2,1)S(1)}, u32[]{:S(2)}) copy-start(bf16[64,16,512]{2,1,0:T(8,128)(2,1)S(1)} %all-to-all-done) | copy-start | bytes 3145732
  113.3 28.0 %all-to-all-start.4 = ((bf16[64,8,768]{2,1,0:T(8,128)(2,1)}), bf16[64,8,768]{2,1,0:T(8,128)(2,1)S(1)}, u32[]{:S(2)}, u32[]{:S(2)}) async-start(bf16[64,8,768]{2,1,0:T(8,128)(2,1)} %copy.80), calls=%async_computation.4 | async-start | bytes 1572864 | tf_op jit(solution)/shard_map/all_to_all | solution.py:48
  121.9 27.7 %copy-start.4 = (bf16[1,768,512]{2,1,0:T(8,128)(2,1)S(1)}, bf16[1,768,512]{2,1,0:T(8,128)(2,1)}, u32[]{:S(2)}) copy-start(bf16[1,768,512]{2,1,0:T(8,128)(2,1)} %param.14) | copy-start | bytes 2359300
  141.3 27.7 %all-to-all-start.2 = ((bf16[64,8,768]{2,1,0:T(8,128)(2,1)}), bf16[64,8,768]{2,1,0:T(8,128)(2,1)S(1)}, u32[]{:S(2)}, u32[]{:S(2)}) async-start(bf16[64,8,768]{2,1,0:T(8,128)(2,1)} %copy.78), calls=%async_computation.2 | async-start | bytes 1572864 | tf_op jit(solution)/shard_map/all_to_all | solution.py:48
  169.0 12.3 %copy-start = (bf16[64,8,768]{2,1,0:T(8,128)(2,1)}, bf16[64,8,768]{2,1,0:T(8,128)(2,1)S(1)}, u32[]{:S(2)}) copy-start(bf16[64,8,768]{2,1,0:T(8,128)(2,1)S(1)} %all-to-all-done.2) | copy-start | bytes 2359300
  169.0 33.4 %all-to-all-start.5 = ((bf16[64,12,512]{2,1,0:T(8,128)(2,1)}), bf16[64,12,512]{2,1,0:T(8,128)(2,1)S(1)}, u32[]{:S(2)}, u32[]{:S(2)}) async-start(bf16[64,12,512]{2,1,0:T(8,128)(2,1)} %reshape_squeeze.11), calls=%async_computation.5 | async-start | bytes 2097152 | tf_op jit(solution)/shard_map/all_to_all | solution.py:36
  177.5 89.1 %all-reduce.3.cloned.1.call-start = ((), (), s32[]{:S(2)}) async-start(), calls=%async_computation.8 | async-start | bytes 6291456 | tf_op jit(solution)/shard_map/psum | solution.py:76
  177.8 3.5 %copy-start.3 = (bf16[64,16,512]{2,1,0:T(8,128)(2,1)S(1)}, bf16[64,16,512]{2,1,0:T(8,128)(2,1)}, u32[]{:S(2)}) copy-start(bf16[64,16,512]{2,1,0:T(8,128)(2,1)} %copy-done.2) | copy-start | bytes 3145732
  270.6 13.2 %copy-start.9 = (f32[128,8]{0,1:T(8,128)S(1)}, f32[128,8]{0,1:T(8,128)}, u32[]{:S(2)}) copy-start(f32[128,8]{0,1:T(8,128)} %param.10) | copy-start | bytes 12292
  270.6 42.5 %all-to-all-start.7 = ((bf16[64,16,512]{2,1,0:T(8,128)(2,1)}), bf16[64,16,512]{2,1,0:T(8,128)(2,1)S(1)}, u32[]{:S(2)}, u32[]{:S(2)}) async-start(bf16[64,16,512]{2,1,0:T(8,128)(2,1)} %bitcast.41), calls=%async_computation.7 | async-start | bytes 2097152 | tf_op jit(solution)/shard_map/all_to_all | solution.py:80
  286.3 29.0 %copy-start.1 = (bf16[64,8,768]{2,1,0:T(8,128)(2,1)S(1)}, bf16[64,8,768]{2,1,0:T(8,128)(2,1)}, u32[]{:S(2)}) copy-start(bf16[64,8,768]{2,1,0:T(8,128)(2,1)} %copy-done) | copy-start | bytes 2359300
Sparse Core Ops, SparseCore 0:
  183.5 83.0 all-reduce.2
where the time goes:
time: 325 us; the launch traced here: 324 us
  waiting for transfers between devices  135 us (42%)
  blocking collectives  71.8 us (22%)
  starting transfers between devices  58.2 us (18%)
  other arithmetic  20.9 us (6%)
  matrix products  15 us (5%)
  between operations  14.3 us (4%)
  local copies, waits for them, and re-layouts  8.53 us (3%)
    all_to_all x1, blocking collectives, shards(): lax.all_to_all(outgoing_parts[1], 'expert', split_axis=0, concat_axis=0,...  38.2 us
    all_to_all x2, waiting for transfers between devices, shards(): lax.all_to_all(shortened(ordered), 'expert', split_axis=0, concat_axis=0,...  36.3 us
    all_to_all x1, blocking collectives, shards(): lax.all_to_all(shortened(ordered), 'expert', split_axis=0, concat_axis=0,...  33.6 us
    psum x1, waiting for transfers between devices, shards(): up_sum = lax.psum(up_part.astype(jnp.bfloat16), 'dp').astype(jnp.float32)  29 us
    all_to_all x1, waiting for transfers between devices, shards(): lax.all_to_all(produced, 'expert', split_axis=0, concat_axis=0, tiled=True)  26.8 us
    all_to_all x1, waiting for transfers between devices, shards(): lax.all_to_all(outgoing, 'expert', split_axis=0, concat_axis=0, tiled=True)  24.1 us
    all_to_all x1, waiting for transfers between devices, shards(): lax.all_to_all(outgoing_parts[2], 'expert', split_axis=0, concat_axis=0,...  19 us
    another operation x3, other arithmetic  18.2 us
  transfers between devices with their start and end apart: 7, of which 6 were waited for; matrix products, arithmetic and copies ran while one was open for 11% of the time, Pallas kernels for 0%

commit v1 on v0

v1 whole, which is shorter than its diff:
```python
import jax
import jax.numpy as jnp
from jax import lax
from jax.experimental import pallas as pl
from jax.experimental.pallas import tpu as pltpu
from jax.sharding import PartitionSpec as P

CAP = 16
LANES = 128
VMEM = pl.BlockSpec(memory_space=pltpu.VMEM)
SMEM = pl.BlockSpec(memory_space=pltpu.SMEM)
F32, BF16, I32 = jnp.float32, jnp.bfloat16, jnp.int32


def call(kernel, out_shape, in_specs, flops=0, moved=0):
    many = isinstance(out_shape, (tuple, list))
    return pl.pallas_call(
        kernel,
        out_shape=out_shape,
        in_specs=in_specs,
        out_specs=[VMEM] * len(out_shape) if many else VMEM,
        compiler_params=pltpu.CompilerParams(vmem_limit_bytes=60 * 1024 * 1024),
        cost_estimate=pl.CostEstimate(flops=flops, bytes_accessed=moved, transcendentals=0),
    )


def dispatch_kernel(ids_ref, keep_ref, map_ref, tokens_ref, out_ref):
    replicas = map_ref.shape[1]
    group = tokens_ref.shape[0]
    ids = jnp.where(keep_ref[...] > 0, ids_ref[...], -1)
    same = lax.broadcasted_iota(I32, (replicas, replicas), 0) == lax.broadcasted_iota(
        I32, (replicas, replicas), 1
    )
    slot_of = jnp.sum(jnp.where(same, map_ref[...], 0), axis=1, keepdims=True)
    wanted = ids[0:1, :] == slot_of
    for k in range(1, ids.shape[0]):
        wanted = wanted | (ids[k : k + 1, :] == slot_of)
    earlier = lax.broadcasted_iota(I32, (group, group), 0) < lax.broadcasted_iota(
        I32, (group, group), 1
    )
    rank = jnp.dot(
        jnp.where(wanted, 1.0, 0.0).astype(BF16),
        jnp.where(earlier, 1.0, 0.0).astype(BF16),
        preferred_element_type=F32,
    )
    place = jnp.where(wanted, rank, -1.0).astype(BF16)
    rows = replicas * CAP
    row = lax.broadcasted_iota(I32, (rows, replicas), 0)
    widen = (row // CAP) == lax.broadcasted_iota(I32, (rows, replicas), 1)
    place = jnp.dot(jnp.where(widen, 1.0, 0.0).astype(BF16), place, preferred_element_type=F32)
    own = (lax.broadcasted_iota(I32, (rows, group), 0) % CAP).astype(F32)
    hits = jnp.where(place == own, 1.0, 0.0).astype(BF16)
    sent = jnp.dot(hits, tokens_ref[...], preferred_element_type=F32).astype(BF16)
    out_ref[...] = sent.reshape(out_ref.shape)


def pack_kernel(gate_ref, up_ref, down_ref, out_ref):
    replicas = out_ref.shape[0]
    half = replicas // 2
    third = out_ref.shape[2] // 3
    for part, ref in enumerate((gate_ref, up_ref)):
        for side in range(2):
            block = ref[:, side * third : (side + 1) * third]
            out_ref[side * half : (side + 1) * half, :, part * third : (part + 1) * third] = (
                block.reshape(half, CAP, third)
            )
    fours = replicas // 4
    for side in range(4):
        block = down_ref[:, side * LANES : (side + 1) * LANES].reshape(fours, 3, CAP, LANES)
        for k in range(3):
            start = 2 * third + k * LANES
            out_ref[side * fours : (side + 1) * fours, :, start : start + LANES] = block[:, k]


def expand_kernel(place_ref, arrived_ref, gate_ref, up_ref, kept_ref, sent_ref):
    core = place_ref[1]
    chips, rows = kept_ref.shape[:2]
    hidden = gate_ref.shape[1]
    for ref, mine in ((sent_ref, 1 - core), (kept_ref, core)):
        for chip in range(chips):
            start = pl.multiple_of((2 * chip + mine) * rows, rows)
            block = arrived_ref[pl.ds(start, rows), :]
            for part, weight_ref in enumerate((gate_ref, up_ref)):
                ref[chip, :, part * hidden : (part + 1) * hidden] = jnp.dot(
                    block, weight_ref[...], preferred_element_type=F32
                ).astype(BF16)


def middle_kernel(place_ref, map_ref, spread_ref, own_ref, other_ref, down_ref, out_ref):
    chip, core = place_ref[0], place_ref[1]
    replicas, _, width = spread_ref.shape
    chips, rows = own_ref.shape[:2]
    groups = rows // CAP

    def move(old, carry):
        out_ref[map_ref[old], :, 0:width] = spread_ref[old]
        return carry

    lax.fori_loop(0, replicas, move, 0, unroll=8)
    for ref, mine in ((own_ref, core), (other_ref, 1 - core)):
        for step in range(chips):
            chunk = 2 * lax.rem(chip + step, chips) + mine
            made = jnp.dot(ref[step], down_ref[...], preferred_element_type=F32).astype(BF16)
            start = pl.multiple_of(chunk * groups, groups)
            out_ref[pl.ds(start, groups), :, width:] = made.reshape(groups, CAP, -1)


def final_kernel(
    ids_ref, keep_ref, gates_ref, map_ref, tokens_ref, landed_ref, mixed_ref, gate_ref, up_ref, down_ref
):
    replicas = map_ref.shape[1]
    group, share = tokens_ref.shape
    half, fours = replicas // 2, replicas // 4
    width = landed_ref.shape[2] - share
    third = width // 3
    for part, ref in enumerate((gate_ref, up_ref)):
        for side in range(2):
            block = landed_ref[
                side * half : (side + 1) * half, :, part * third : (part + 1) * third
            ]
            ref[:, side * third : (side + 1) * third] = block.reshape(half * CAP, third)
    for side in range(4):
        blocks = [
            landed_ref[
                side * fours : (side + 1) * fours,
                :,
                2 * third + k * LANES : 2 * third + (k + 1) * LANES,
            ].reshape(fours, 1, CAP, LANES)
            for k in range(3)
        ]
        down_ref[:, side * LANES : (side + 1) * LANES] = jnp.concatenate(blocks, axis=1).reshape(
            fours * 3 * CAP, LANES
        )

    ids = jnp.where(keep_ref[...] > 0, ids_ref[...], -1).T
    gates = gates_ref[...].T
    slot_of = map_ref[...]
    hits = [ids[:, k : k + 1] == slot_of for k in range(ids.shape[1])]
    wanted, weight = hits[0], jnp.where(hits[0], gates[:, 0:1], 0.0)
    for k in range(1, ids.shape[1]):
        wanted = wanted | hits[k]
        weight = weight + jnp.where(hits[k], gates[:, k : k + 1], 0.0)
    earlier = lax.broadcasted_iota(I32, (group, group), 1) < lax.broadcasted_iota(
        I32, (group, group), 0
    )
    rank = jnp.dot(
        jnp.where(earlier, 1.0, 0.0).astype(BF16),
        jnp.where(wanted, 1.0, 0.0).astype(BF16),
        preferred_element_type=F32,
    )
    place = jnp.where(wanted, rank, -1.0).astype(BF16)
    rows = replicas * CAP
    widen = lax.broadcasted_iota(I32, (replicas, rows), 0) == (
        lax.broadcasted_iota(I32, (replicas, rows), 1) // CAP
    )
    widen = jnp.where(widen, 1.0, 0.0).astype(BF16)
    place = jnp.dot(place, widen, preferred_element_type=F32)
    match = place == (lax.broadcasted_iota(I32, (group, rows), 1) % CAP).astype(F32)
    returned = landed_ref[:, :, width:].reshape(rows, share)
    total = tokens_ref[...].astype(F32)
    left = weight
    for _ in range(3):
        top = left.astype(BF16)
        left = left - top.astype(F32)
        spread = jnp.dot(top, widen, preferred_element_type=F32)
        factor = jnp.where(match, spread, 0.0).astype(BF16)
        total = total + jnp.dot(factor, returned, preferred_element_type=F32)
    mixed_ref[...] = total.astype(BF16)


def exchange(parts):
    return lax.all_to_all(parts, "expert", split_axis=0, concat_axis=0, tiled=True)


def hop(value, to):
    places = [(d, to(d // 2, d % 2)) for d in range(lax.axis_size("dp"))]
    return lax.ppermute(value, "dp", [(d, 2 * chip + core) for d, (chip, core) in places])


def pick(values, index):
    return lax.dynamic_index_in_dim(values, index, axis=0, keepdims=False)


def shards(tokens, route_ids, route_gates, keep_mask, old_gate, old_up, old_down, placement_map):
    replicas = lax.axis_size("expert")
    chips = lax.axis_size("dp") // 2
    share = tokens.shape[1]
    hidden_size = old_gate.shape[2]
    gate_local, up_local, down_local = old_gate[0], old_up[0], old_down[0]
    position = lax.axis_index("dp")
    chip, core = position // 2, position % 2
    place = jnp.stack([chip, core]).astype(I32)
    map_row = placement_map.reshape(1, replicas)
    width = 3 * share * hidden_size // (replicas * CAP)
    rows = replicas * CAP

    outgoing = call(
        dispatch_kernel,
        jax.ShapeDtypeStruct((replicas, CAP, share), BF16),
        [VMEM] * 4,
    )(route_ids.T, keep_mask.T, map_row, tokens)
    received = exchange(outgoing)

    pieces = call(
        pack_kernel, jax.ShapeDtypeStruct((replicas, CAP, width), BF16), [VMEM] * 3
    )(gate_local, up_local, down_local)
    pieces, received = lax.optimization_barrier((pieces, received))
    spread = exchange(pieces)

    piece_rows = rows // (2 * chips)
    part = jax.ShapeDtypeStruct((chips, piece_rows, 2 * hidden_size), BF16)
    kept, sent = call(
        expand_kernel,
        (part, part),
        [SMEM, VMEM, VMEM, VMEM],
        flops=4 * rows * share * hidden_size,
        moved=8 << 20,
    )(place, received.reshape(rows, share), gate_local, up_local)

    flip = lambda c: c ^ 1
    mirror = lambda c: chips - 1 - c
    pair = kept.astype(F32) + hop(sent, lambda c, k: (c, 1 - k)).astype(F32)
    pair = pair.astype(BF16)
    gates, ups = pair[:, :, :hidden_size], pair[:, :, hidden_size:]
    beside, across = flip(chip), mirror(chip)
    diagonal = flip(across)
    gate_sent = jnp.stack([pick(gates, beside), pick(gates, diagonal)])
    up_sent = jnp.stack([pick(ups, across), pick(ups, diagonal)])
    gate_got = hop(gate_sent, lambda c, k: (flip(c), k)).astype(F32)
    up_got = hop(up_sent, lambda c, k: (mirror(c), k)).astype(F32)
    gate_second = (pick(gates, across).astype(F32) + gate_got[1]).astype(BF16)
    up_second = (pick(ups, beside).astype(F32) + up_got[1]).astype(BF16)
    gate_last = hop(gate_second, lambda c, k: (mirror(c), k)).astype(F32)
    up_last = hop(up_second, lambda c, k: (flip(c), k)).astype(F32)
    gate_sum = pick(gates, chip).astype(F32) + gate_got[0] + gate_last
    up_sum = pick(ups, chip).astype(F32) + up_got[0] + up_last
    hidden = (jax.nn.silu(gate_sum) * up_sum).astype(BF16)
    own = jnp.stack(
        [hidden]
        + [hop(hidden, lambda c, k, s=s: ((c - s) % chips, k)) for s in range(1, chips)]
    )
    other = hop(own, lambda c, k: (c, 1 - k))

    joined = call(
        middle_kernel,
        jax.ShapeDtypeStruct((replicas, CAP, width + share), BF16),
        [SMEM, SMEM, VMEM, VMEM, VMEM, VMEM],
    )(place, placement_map, spread, own, other, down_local)
    landed = exchange(joined)

    mixed, new_gate, new_up, new_down = call(
        final_kernel,
        tuple(
            jax.ShapeDtypeStruct(a.shape, BF16) for a in (tokens, gate_local, up_local, down_local)
        ),
        [VMEM] * 6,
    )(route_ids.T, keep_mask.T, route_gates.T, map_row, tokens, landed)
    return (mixed, new_gate[None], new_up[None], new_down[None])


def solution(mesh):
    in_specs = (
        P("expert", "dp"),
        P("expert", None),
        P("expert", None),
        P("expert", None),
        P("expert", "dp", None),
        P("expert", "dp", None),
        P("expert", None, "dp"),
        P(),
    )
    out_specs = (
        P("expert", "dp"),
        P("expert", "dp", None),
        P("expert", "dp", None),
        P("expert", None, "dp"),
    )
    return jax.shard_map(shards, mesh=mesh, in_specs=in_specs, out_specs=out_specs, check_vma=False)
```

time: 325 us -> 227 us (0.70)
  waiting for transfers between devices: 135 us -> 53.7 us
  Pallas kernels: 0 us -> 21.1 us
  blocking collectives: 71.8 us -> 90.7 us
  other arithmetic: 20.9 us -> 4.86 us
  matrix products: 15 us -> 0 us
  between operations: 14.3 us -> 0.91 us
  starting transfers between devices: 58.2 us -> 47.8 us
  local copies, waits for them, and re-layouts: 8.53 us -> 4.31 us
    all_to_all x6 -> x2, waiting for transfers between devices: 106 us -> 28.3 us  [exchange(): lax.all_to_all(parts, 'expert', split_axis=0, concat_axis=0, tiled=True)]
    all_to_all x6 -> x2, starting transfers between devices: 58 us -> 22.4 us  [exchange(): lax.all_to_all(parts, 'expert', split_axis=0, concat_axis=0, tiled=True)]
    psum x1 -> x0, waiting for transfers between devices: 29 us -> none  [shards(): up_sum = lax.psum(up_part.astype(jnp.bfloat16), 'dp').astype(jnp.float32)]
    ppermute x0 -> x9, waiting for transfers between devices: none -> 25.4 us  [hop(): lax.ppermute(value, 'dp', [(d, 2 * chip + core) for d, (chip, core) in pl...]
    ppermute x0 -> x9, starting transfers between devices: none -> 25.4 us  [hop(): lax.ppermute(value, 'dp', [(d, 2 * chip + core) for d, (chip, core) in pl...]
    pallas_call x0 -> x5, Pallas kernels: none -> 21.1 us  [the longest x1 5.25 us: shards(): call(middle_kernel, jax.ShapeDtypeStruct((replicas, CAP, width + share),...]
    all_to_all x2 -> x1, blocking collectives: 71.8 us -> 90.7 us  [exchange(): lax.all_to_all(parts, 'expert', split_axis=0, concat_axis=0, tiled=True)]
    another operation x3 -> x4, other arithmetic: 18.2 us -> 0.83 us  [the longest x1 0.65 us: shards(): place = jnp.stack([chip, core]).astype(I32)]
  transfers between devices with their start and end apart: 7 -> 11, of which waited for: 6 -> 8; matrix products, arithmetic and copies ran while one was open for 11% -> 2% of each run, Pallas kernels for 0% -> 1%
where the time goes in v1:
time: 227 us; the launch traced here: 223 us
  blocking collectives  90.7 us (40%)
  waiting for transfers between devices  53.7 us (24%)
  starting transfers between devices  47.8 us (21%)
  Pallas kernels  21.1 us (9%)
  other arithmetic  4.86 us (2%)
  local copies, waits for them, and re-layouts  4.31 us (2%)
    all_to_all x1, blocking collectives, exchange(): lax.all_to_all(parts, 'expert', split_axis=0, concat_axis=0, tiled=True)  90.7 us
    all_to_all x2, waiting for transfers between devices, exchange(): lax.all_to_all(parts, 'expert', split_axis=0, concat_axis=0, tiled=True)  28.3 us
    ppermute x9, waiting for transfers between devices, hop(): lax.ppermute(value, 'dp', [(d, 2 * chip + core) for d, (chip, core) in pl...  25.4 us
    ppermute x9, starting transfers between devices, hop(): lax.ppermute(value, 'dp', [(d, 2 * chip + core) for d, (chip, core) in pl...  25.4 us
    all_to_all x2, starting transfers between devices, exchange(): lax.all_to_all(parts, 'expert', split_axis=0, concat_axis=0, tiled=True)  22.4 us
    pallas_call x1, Pallas kernels, shards(): call(middle_kernel, jax.ShapeDtypeStruct((replicas, CAP, width + share),...  5.25 us
    pallas_call x1, Pallas kernels, shards(): call(final_kernel, tuple((jax.ShapeDtypeStruct(a.shape, BF16) for a in (t...  5.15 us
    pallas_call x1, Pallas kernels, shards(): call(expand_kernel, (part, part), [SMEM, VMEM, VMEM, VMEM], flops=4 * row...  4.65 us
  transfers between devices with their start and end apart: 11, of which 8 were waited for; matrix products, arithmetic and copies ran while one was open for 2% of the time, Pallas kernels for 1%

profile of v1, /device:TPU:7, one launch (start us, length us, event | category | flops | bytes accessed | tf_op | source)
XLA Modules:
  0.0 223.4 jit_solution(12168987572075448421)
XLA Ops:
  0.6 2.7 %shard_map.112 = bf16[64,16,512]{2,1,0:T(8,128)(2,1)} custom-call(s32[8,128]{1,0:T(8,128)} %bitcast.46, s32[8,128]{1,0:T(8,128)} %bitcast.48, s32[1,64]{1,0:T(1,128)} %bitcast.50, bf16[128,512]{1,0:T(8,128)(2,1)} %tokens_ref.3), custom_call_target="tpu_custom_call" | custom-call | tf_op jit(solution)/shard_map/pallas_call | solution.py:197
  3.4 16.3 %all-to-all-start = ((bf16[64,16,512]{2,1,0:T(8,128)(2,1)}), bf16[64,16,512]{2,1,0:T(8,128)(2,1)S(1)}, u32[]{:S(2)}, u32[]{:S(2)}) async-start(bf16[64,16,512]{2,1,0:T(8,128)(2,1)} %shard_map.112), calls=%async_computation | async-start | bytes 2097152 | tf_op jit(solution)/shard_map/all_to_all | solution.py:172
  19.7 3.3 %shard_map.111 = bf16[64,16,1152]{2,1,0:T(8,128)(2,1)} custom-call(bf16[512,768]{1,0:T(8,128)(2,1)} %bitcast.38, bf16[512,768]{1,0:T(8,128)(2,1)} %bitcast.40, bf16[768,512]{1,0:T(8,128)(2,1)} %bitcast.35), custom_call_target="tpu_custom_call" | custom-call | tf_op jit(solution)/shard_map/pallas_call | solution.py:204
  23.0 0.7 pad_add_fusion.place_ref
  23.7 23.4 %all-to-all-done = bf16[64,16,512]{2,1,0:T(8,128)(2,1)S(1)} async-done(((bf16[64,16,512]{2,1,0:T(8,128)(2,1)}), bf16[64,16,512]{2,1,0:T(8,128)(2,1)S(1)}, u32[]{:S(2)}, u32[]{:S(2)}) %all-to-all-start) | async-done | bytes 1048608 | tf_op jit(solution)/shard_map/all_to_all | solution.py:172
  47.1 0.0 copy-start.5
  47.1 1.0 copy-done.5
  48.1 4.7 %shard_map.113 = (bf16[4,128,1536]{2,1,0:T(8,128)(2,1)}, bf16[4,128,1536]{2,1,0:T(8,128)(2,1)}) custom-call(s32[2]{0:T(128)} %pad_add_fusion.place_ref, bf16[1024,512]{1,0:T(8,128)(2,1)} %bitcast.37, bf16[512,768]{1,0:T(8,128)(2,1)} %bitcast.39, bf16[512,768]{1,0:T(8,128)(2,1)} %bitcast.41), custom_call_target="tpu_custom_call" | custom-call | flops 1610612736 | bytes 8388608 | tf_op jit(solution)/shard_map/pallas_call | solution.py:212
  52.8 5.2 %collective-permute-start = (bf16[4,128,1536]{2,1,0:T(8,128)(2,1)}, bf16[4,128,1536]{2,1,0:T(8,128)(2,1)}, u32[]{:S(2)}, u32[]{:S(2)}) collective-permute-start(bf16[4,128,1536]{2,1,0:T(8,128)(2,1)} %get-tuple-element.15), channel_id=1, source_target_pairs={{0,1},{1,0},{2,3},{3,2},{4,5},{5,4},{6,7},{7,6},{8,9},{9,8},{10,11... | collective-permute-start | bytes 4718600 | tf_op jit(solution)/shard_map/ppermute | solution.py:177
  58.0 6.1 %all-to-all-start.1 = ((bf16[64,16,1152]{2,1,0:T(8,128)(2,1)}), bf16[64,16,1152]{2,1,0:T(8,128)(2,1)S(1)}, u32[]{:S(2)}, u32[]{:S(2)}) async-start(bf16[64,16,1152]{2,1,0:T(8,128)(2,1)} %shard_map.111), calls=%async_computation.1 | async-start | bytes 4718592 | tf_op jit(solution)/shard_map/all_to_all | solution.py:172
  64.1 0.0 collective-permute-done
  64.2 2.3 %add_convert_fusion = bf16[4,128,1536]{2,1,0:T(8,128)(2,1)S(1)} fusion(bf16[4,128,1536]{2,1,0:T(8,128)(2,1)} %collective-permute-done, bf16[4,128,1536]{2,1,0:T(8,128)(2,1)} %get-tuple-element.14), kind=kLoop, calls=%fused_computation | loop fusion | flops 3145728 | bytes 4718592 | tf_op jit(solution)/shard_map/convert_element_type | solution.py:223
  66.4 0.1 fusion.10
  66.5 0.0 copy-start.2
  66.7 2.1 collective-permute-start.3
  68.9 2.5 %collective-permute-start.1 = (bf16[2,128,768]{2,1,0:T(8,128)(2,1)S(1)}, bf16[2,128,768]{2,1,0:T(8,128)(2,1)S(1)}, u32[]{:S(2)}, u32[]{:S(2)}) collective-permute-start(bf16[2,128,768]{2,1,0:T(8,128)(2,1)S(1)} %pad_maximum_fusion.1), channel_id=1, source_target_pairs={{0,2},{1,3},{2,0},{3,1},{4,6},{5,7},{6,4},{7,5},{8,10},{9,11},{10,... | collective-permute-start | bytes 1179656 | tf_op jit(solution)/shard_map/ppermute | solution.py:177
  71.4 8.8 %collective-permute-done.3 = bf16[2,128,768]{2,1,0:T(8,128)(2,1)S(1)} collective-permute-done((bf16[2,128,768]{2,1,0:T(8,128)(2,1)S(1)}, bf16[2,128,768]{2,1,0:T(8,128)(2,1)S(1)}, u32[]{:S(2)}, u32[]{:S(2)}) %collective-permute-start.3) | collective-permute-done | bytes 393248 | tf_op jit(solution)/shard_map/ppermute | solution.py:177
  80.2 0.1 convert_element_type.62
  80.2 0.0 copy-done.2
  80.2 0.0 copy-start.3
  80.3 0.1 fusion.9
  80.3 0.8 copy-done.3
  81.1 1.9 collective-permute-start.4
  83.0 0.0 collective-permute-done.1
  83.1 0.1 convert_element_type.56
  83.1 0.0 copy-start.4
  83.1 0.9 copy-done.4
  84.0 2.2 collective-permute-start.2
  86.2 2.2 collective-permute-done.4
  88.4 4.1 %collective-permute-done.2 = bf16[128,768]{1,0:T(8,128)(2,1)} collective-permute-done((bf16[128,768]{1,0:T(8,128)(2,1)S(1)}, bf16[128,768]{1,0:T(8,128)(2,1)}, u32[]{:S(2)}, u32[]{:S(2)}) %collective-permute-start.2) | collective-permute-done | bytes 196640 | tf_op jit(solution)/shard_map/ppermute | solution.py:177
  92.5 1.6 fusion.4
  94.1 1.9 collective-permute-start.7
  96.0 3.6 %collective-permute-start.6 = (bf16[128,768]{1,0:T(8,128)(2,1)S(1)}, bf16[128,768]{1,0:T(8,128)(2,1)S(1)}, u32[]{:S(2)}, u32[]{:S(2)}) collective-permute-start(bf16[128,768]{1,0:T(8,128)(2,1)S(1)} %fusion.4), channel_id=1, source_target_pairs={{0,4},{1,5},{2,6},{3,7},{4,0},{5,1},{6,2},{7,3},{8,12},{9,13},{10,... | collective-permute-start | bytes 589832 | tf_op jit(solution)/shard_map/ppermute | solution.py:177
  99.7 1.9 collective-permute-start.5
  101.6 0.0 collective-permute-done.7
  101.6 2.6 %collective-permute-done.6 = bf16[128,768]{1,0:T(8,128)(2,1)S(1)} collective-permute-done((bf16[128,768]{1,0:T(8,128)(2,1)S(1)}, bf16[128,768]{1,0:T(8,128)(2,1)S(1)}, u32[]{:S(2)}, u32[]{:S(2)}) %collective-permute-start.6) | collective-permute-done | bytes 196640 | tf_op jit(solution)/shard_map/ppermute | solution.py:177
  104.2 5.6 %collective-permute-done.5 = bf16[128,768]{1,0:T(8,128)(2,1)S(1)} collective-permute-done((bf16[128,768]{1,0:T(8,128)(2,1)S(1)}, bf16[128,768]{1,0:T(8,128)(2,1)S(1)}, u32[]{:S(2)}, u32[]{:S(2)}) %collective-permute-start.5) | collective-permute-done | bytes 196640 | tf_op jit(solution)/shard_map/ppermute | solution.py:177
  109.9 0.1 pad_maximum_fusion.own_ref
  110.0 0.0 copy-start.1
  110.0 3.9 %collective-permute-start.8 = (bf16[4,128,768]{2,1,0:T(8,128)(2,1)S(1)}, bf16[4,128,768]{2,1,0:T(8,128)(2,1)}, u32[]{:S(2)}, u32[]{:S(2)}) collective-permute-start(bf16[4,128,768]{2,1,0:T(8,128)(2,1)S(1)} %pad_maximum_fusion.own_ref), channel_id=1, source_target_pairs={{0,1},{1,0},{2,3},{3,2},{4,5},{5,4},{6,7},{7,6},{8,9},{9,8},{10,11... | collective-permute-start | bytes 2359304 | tf_op jit(solution)/shard_map/ppermute | solution.py:177
  113.9 2.0 collective-permute-done.8.other_ref
  115.9 4.9 %all-to-all-done.1.spread_ref = bf16[64,16,1152]{2,1,0:T(8,128)(2,1)S(1)} async-done(((bf16[64,16,1152]{2,1,0:T(8,128)(2,1)}), bf16[64,16,1152]{2,1,0:T(8,128)(2,1)S(1)}, u32[]{:S(2)}, u32[]{:S(2)}) %all-to-all-start.1) | async-done | bytes 2359328 | tf_op jit(solution)/shard_map/all_to_all | solution.py:172
  120.8 0.0 copy-done.1
  120.8 0.0 copy-start
  120.8 1.4 copy-done
  122.2 5.3 %shard_map.114 = bf16[64,16,1664]{2,1,0:T(8,128)(2,1)} custom-call(s32[2]{0:T(128)} %pad_add_fusion.place_ref, s32[64]{0:T(128)} %map_ref.1, bf16[64,16,1152]{2,1,0:T(8,128)(2,1)} %copy-done, bf16[4,128,768]{2,1,0:T(8,128)(2,1)} %copy-done.1, bf16[4,128,768]{2,1,0:T(8,128)(2,1)} %collective-permute-done.8.other_ref, bf16[768,512]{1,0:T(8,128)(2,1)} %bitcast.36), custom_call_target="tpu_custom_call" | custom-call | tf_op jit(solution)/shard_map/pallas_call | solution.py:244
  127.5 90.7 %all_to_all.15.landed_ref = bf16[64,16,1664]{2,1,0:T(8,128)(2,1)} all-to-all(bf16[64,16,1664]{2,1,0:T(8,128)(2,1)} %shard_map.114), channel_id=1, replica_groups=mesh['expert'=64,'dp'=8] {'expert'}, dimensions={0} | all-to-all | bytes 6815744 | tf_op jit(solution)/shard_map/all_to_all | solution.py:172
  218.2 5.2 %shard_map.115 = (bf16[128,512]{1,0:T(8,128)(2,1)}, bf16[512,768]{1,0:T(8,128)(2,1)}, bf16[512,768]{1,0:T(8,128)(2,1)}, bf16[768,512]{1,0:T(8,128)(2,1)}) custom-call(s32[8,128]{1,0:T(8,128)} %bitcast.47, s32[8,128]{1,0:T(8,128)} %bitcast.49, f32[8,128]{1,0:T(8,128)} %bitcast.52, s32[1,64]{1,0:T(1,128)} %bitcast.51, bf16[128,512]{1,0:T(8,128)(2,1)} %tokens_ref.3, ...), custom_call_target="tpu_custom_call" | custom-call | tf_op jit(solution)/shard_map/pallas_call | solution.py:251
  (5 shorter events, 0.2 us)
Async XLA Ops:
  3.4 43.7 %all-to-all-start = ((bf16[64,16,512]{2,1,0:T(8,128)(2,1)}), bf16[64,16,512]{2,1,0:T(8,128)(2,1)S(1)}, u32[]{:S(2)}, u32[]{:S(2)}) async-start(bf16[64,16,512]{2,1,0:T(8,128)(2,1)} %shard_map.112), calls=%async_computation | async-start | bytes 2097152 | tf_op jit(solution)/shard_map/all_to_all | solution.py:172
  47.1 1.0 copy-start.5
  52.8 11.4 %collective-permute-start = (bf16[4,128,1536]{2,1,0:T(8,128)(2,1)}, bf16[4,128,1536]{2,1,0:T(8,128)(2,1)}, u32[]{:S(2)}, u32[]{:S(2)}) collective-permute-start(bf16[4,128,1536]{2,1,0:T(8,128)(2,1)} %get-tuple-element.15), channel_id=1, source_target_pairs={{0,1},{1,0},{2,3},{3,2},{4,5},{5,4},{6,7},{7,6},{8,9},{9,8},{10,11... | collective-permute-start | bytes 4718600 | tf_op jit(solution)/shard_map/ppermute | solution.py:177
  58.0 62.8 %all-to-all-start.1 = ((bf16[64,16,1152]{2,1,0:T(8,128)(2,1)}), bf16[64,16,1152]{2,1,0:T(8,128)(2,1)S(1)}, u32[]{:S(2)}, u32[]{:S(2)}) async-start(bf16[64,16,1152]{2,1,0:T(8,128)(2,1)} %shard_map.111), calls=%async_computation.1 | async-start | bytes 4718592 | tf_op jit(solution)/shard_map/all_to_all | solution.py:172
  66.5 13.7 %copy-start.2 = (bf16[4,128,768]{2,1,0:T(8,128)(2,1)}, bf16[4,128,768]{2,1,0:T(8,128)(2,1)S(1)}, u32[]{:S(2)}) copy-start(bf16[4,128,768]{2,1,0:T(8,128)(2,1)S(1)} %get-tuple-element.21) | copy-start | bytes 2359300
  66.7 13.5 %collective-permute-start.3 = (bf16[2,128,768]{2,1,0:T(8,128)(2,1)S(1)}, bf16[2,128,768]{2,1,0:T(8,128)(2,1)S(1)}, u32[]{:S(2)}, u32[]{:S(2)}) collective-permute-start(bf16[2,128,768]{2,1,0:T(8,128)(2,1)S(1)} %pad_maximum_fusion.2), channel_id=1, source_target_pairs={{0,6},{1,7},{2,4},{3,5},{4,2},{5,3},{6,0},{7,1},{8,14},{9,15},{10,... | collective-permute-start | bytes 1179656 | tf_op jit(solution)/shard_map/ppermute | solution.py:177
  68.9 14.2 %collective-permute-start.1 = (bf16[2,128,768]{2,1,0:T(8,128)(2,1)S(1)}, bf16[2,128,768]{2,1,0:T(8,128)(2,1)S(1)}, u32[]{:S(2)}, u32[]{:S(2)}) collective-permute-start(bf16[2,128,768]{2,1,0:T(8,128)(2,1)S(1)} %pad_maximum_fusion.1), channel_id=1, source_target_pairs={{0,2},{1,3},{2,0},{3,1},{4,6},{5,7},{6,4},{7,5},{8,10},{9,11},{10,... | collective-permute-start | bytes 1179656 | tf_op jit(solution)/shard_map/ppermute | solution.py:177
  80.2 0.9 copy-start.3
  81.1 7.3 %collective-permute-start.4 = (bf16[128,768]{1,0:T(8,128)(2,1)S(1)}, bf16[128,768]{1,0:T(8,128)(2,1)}, u32[]{:S(2)}, u32[]{:S(2)}) collective-permute-start(bf16[128,768]{1,0:T(8,128)(2,1)S(1)} %fusion.9), channel_id=1, source_target_pairs={{0,2},{1,3},{2,0},{3,1},{4,6},{5,7},{6,4},{7,5},{8,10},{9,11},{10,... | collective-permute-start | bytes 589832 | tf_op jit(solution)/shard_map/ppermute | solution.py:177
  83.1 0.9 copy-start.4
  84.0 8.5 %collective-permute-start.2 = (bf16[128,768]{1,0:T(8,128)(2,1)S(1)}, bf16[128,768]{1,0:T(8,128)(2,1)}, u32[]{:S(2)}, u32[]{:S(2)}) collective-permute-start(bf16[128,768]{1,0:T(8,128)(2,1)S(1)} %fusion.8), channel_id=1, source_target_pairs={{0,6},{1,7},{2,4},{3,5},{4,2},{5,3},{6,0},{7,1},{8,14},{9,15},{10,... | collective-permute-start | bytes 589832 | tf_op jit(solution)/shard_map/ppermute | solution.py:177
  94.1 7.5 %collective-permute-start.7 = (bf16[128,768]{1,0:T(8,128)(2,1)S(1)}, bf16[128,768]{1,0:T(8,128)(2,1)S(1)}, u32[]{:S(2)}, u32[]{:S(2)}) collective-permute-start(bf16[128,768]{1,0:T(8,128)(2,1)S(1)} %fusion.4), channel_id=1, source_target_pairs={{0,2},{1,3},{2,4},{3,5},{4,6},{5,7},{6,0},{7,1},{8,10},{9,11},{10,... | collective-permute-start | bytes 589832 | tf_op jit(solution)/shard_map/ppermute | solution.py:177
  96.0 8.2 %collective-permute-start.6 = (bf16[128,768]{1,0:T(8,128)(2,1)S(1)}, bf16[128,768]{1,0:T(8,128)(2,1)S(1)}, u32[]{:S(2)}, u32[]{:S(2)}) collective-permute-start(bf16[128,768]{1,0:T(8,128)(2,1)S(1)} %fusion.4), channel_id=1, source_target_pairs={{0,4},{1,5},{2,6},{3,7},{4,0},{5,1},{6,2},{7,3},{8,12},{9,13},{10,... | collective-permute-start | bytes 589832 | tf_op jit(solution)/shard_map/ppermute | solution.py:177
  99.7 10.2 %collective-permute-start.5 = (bf16[128,768]{1,0:T(8,128)(2,1)S(1)}, bf16[128,768]{1,0:T(8,128)(2,1)S(1)}, u32[]{:S(2)}, u32[]{:S(2)}) collective-permute-start(bf16[128,768]{1,0:T(8,128)(2,1)S(1)} %fusion.4), channel_id=1, source_target_pairs={{0,6},{1,7},{2,0},{3,1},{4,2},{5,3},{6,4},{7,5},{8,14},{9,15},{10,... | collective-permute-start | bytes 589832 | tf_op jit(solution)/shard_map/ppermute | solution.py:177
  110.0 10.9 %copy-start.1 = (bf16[4,128,768]{2,1,0:T(8,128)(2,1)}, bf16[4,128,768]{2,1,0:T(8,128)(2,1)S(1)}, u32[]{:S(2)}) copy-start(bf16[4,128,768]{2,1,0:T(8,128)(2,1)S(1)} %pad_maximum_fusion.own_ref) | copy-start | bytes 2359300
  110.0 6.0 %collective-permute-start.8 = (bf16[4,128,768]{2,1,0:T(8,128)(2,1)S(1)}, bf16[4,128,768]{2,1,0:T(8,128)(2,1)}, u32[]{:S(2)}, u32[]{:S(2)}) collective-permute-start(bf16[4,128,768]{2,1,0:T(8,128)(2,1)S(1)} %pad_maximum_fusion.own_ref), channel_id=1, source_target_pairs={{0,1},{1,0},{2,3},{3,2},{4,5},{5,4},{6,7},{7,6},{8,9},{9,8},{10,11... | collective-permute-start | bytes 2359304 | tf_op jit(solution)/shard_map/ppermute | solution.py:177
  120.8 1.4 copy-start

commit v2 on v1

--- a/solution.py
+++ b/solution.py
@@ -9,18 +9,19 @@
 LANES = 128
 VMEM = pl.BlockSpec(memory_space=pltpu.VMEM)
 SMEM = pl.BlockSpec(memory_space=pltpu.SMEM)
+ANY = pl.BlockSpec(memory_space=pl.ANY)
 F32, BF16, I32 = jnp.float32, jnp.bfloat16, jnp.int32
 
 
-def call(kernel, out_shape, in_specs, flops=0, moved=0):
+def call(kernel, out_shape, in_specs, limit=60, **more):
     many = isinstance(out_shape, (tuple, list))
+    more.setdefault("out_specs", [VMEM] * len(out_shape) if many else VMEM)
     return pl.pallas_call(
         kernel,
         out_shape=out_shape,
         in_specs=in_specs,
-        out_specs=[VMEM] * len(out_shape) if many else VMEM,
-        compiler_params=pltpu.CompilerParams(vmem_limit_bytes=60 * 1024 * 1024),
-        cost_estimate=pl.CostEstimate(flops=flops, bytes_accessed=moved, transcendentals=0),
+        compiler_params=pltpu.CompilerParams(vmem_limit_bytes=limit * 1024 * 1024),
+        **more,
     )
 
 
@@ -72,66 +73,33 @@
             out_ref[side * fours : (side + 1) * fours, :, start : start + LANES] = block[:, k]
 
 
-def expand_kernel(place_ref, arrived_ref, gate_ref, up_ref, kept_ref, sent_ref):
-    core = place_ref[1]
-    chips, rows = kept_ref.shape[:2]
+def expand_kernel(place_ref, arrived_ref, gate_ref, up_ref, out_ref):
+    chips, rows = out_ref.shape[:2]
     hidden = gate_ref.shape[1]
-    for ref, mine in ((sent_ref, 1 - core), (kept_ref, core)):
-        for chip in range(chips):
-            start = pl.multiple_of((2 * chip + mine) * rows, rows)
-            block = arrived_ref[pl.ds(start, rows), :]
-            for part, weight_ref in enumerate((gate_ref, up_ref)):
-                ref[chip, :, part * hidden : (part + 1) * hidden] = jnp.dot(
-                    block, weight_ref[...], preferred_element_type=F32
-                ).astype(BF16)
-
-
-def middle_kernel(place_ref, map_ref, spread_ref, own_ref, other_ref, down_ref, out_ref):
+    for chip in range(chips):
+        start = pl.multiple_of((2 * chip + place_ref[0]) * rows, rows)
+        block = arrived_ref[pl.ds(start, rows), :]
+        for part, weight_ref in enumerate((gate_ref, up_ref)):
+            out_ref[chip, :, part * hidden : (part + 1) * hidden] = jnp.dot(
+                block, weight_ref[...], preferred_element_type=F32
+            ).astype(BF16)
+
+
+def produce_kernel(
+    place_ref, own_ref, other_ref, down_ref, ids_ref, keep_ref, gates_ref, map_ref, made_ref, factor_ref
+):
     chip, core = place_ref[0], place_ref[1]
-    replicas, _, width = spread_ref.shape
     chips, rows = own_ref.shape[:2]
     groups = rows // CAP
-
-    def move(old, carry):
-        out_ref[map_ref[old], :, 0:width] = spread_ref[old]
-        return carry
-
-    lax.fori_loop(0, replicas, move, 0, unroll=8)
     for ref, mine in ((own_ref, core), (other_ref, 1 - core)):
         for step in range(chips):
             chunk = 2 * lax.rem(chip + step, chips) + mine
             made = jnp.dot(ref[step], down_ref[...], preferred_element_type=F32).astype(BF16)
             start = pl.multiple_of(chunk * groups, groups)
-            out_ref[pl.ds(start, groups), :, width:] = made.reshape(groups, CAP, -1)
-
-
-def final_kernel(
-    ids_ref, keep_ref, gates_ref, map_ref, tokens_ref, landed_ref, mixed_ref, gate_ref, up_ref, down_ref
-):
+            made_ref[pl.ds(start, groups)] = made.reshape(groups, CAP, -1)
+
     replicas = map_ref.shape[1]
-    group, share = tokens_ref.shape
-    half, fours = replicas // 2, replicas // 4
-    width = landed_ref.shape[2] - share
-    third = width // 3
-    for part, ref in enumerate((gate_ref, up_ref)):
-        for side in range(2):
-            block = landed_ref[
-                side * half : (side + 1) * half, :, part * third : (part + 1) * third
-            ]
-            ref[:, side * third : (side + 1) * third] = block.reshape(half * CAP, third)
-    for side in range(4):
-        blocks = [
-            landed_ref[
-                side * fours : (side + 1) * fours,
-                :,
-                2 * third + k * LANES : 2 * third + (k + 1) * LANES,
-            ].reshape(fours, 1, CAP, LANES)
-            for k in range(3)
-        ]
-        down_ref[:, side * LANES : (side + 1) * LANES] = jnp.concatenate(blocks, axis=1).reshape(
-            fours * 3 * CAP, LANES
-        )
-
+    group = ids_ref.shape[1]
     ids = jnp.where(keep_ref[...] > 0, ids_ref[...], -1).T
     gates = gates_ref[...].T
     slot_of = map_ref[...]
@@ -149,23 +117,68 @@
         preferred_element_type=F32,
     )
     place = jnp.where(wanted, rank, -1.0).astype(BF16)
-    rows = replicas * CAP
-    widen = lax.broadcasted_iota(I32, (replicas, rows), 0) == (
-        lax.broadcasted_iota(I32, (replicas, rows), 1) // CAP
+    width = replicas * CAP
+    widen = lax.broadcasted_iota(I32, (replicas, width), 0) == (
+        lax.broadcasted_iota(I32, (replicas, width), 1) // CAP
     )
     widen = jnp.where(widen, 1.0, 0.0).astype(BF16)
     place = jnp.dot(place, widen, preferred_element_type=F32)
-    match = place == (lax.broadcasted_iota(I32, (group, rows), 1) % CAP).astype(F32)
-    returned = landed_ref[:, :, width:].reshape(rows, share)
-    total = tokens_ref[...].astype(F32)
+    match = place == (lax.broadcasted_iota(I32, (group, width), 1) % CAP).astype(F32)
     left = weight
-    for _ in range(3):
+    for term in range(factor_ref.shape[0]):
         top = left.astype(BF16)
         left = left - top.astype(F32)
         spread = jnp.dot(top, widen, preferred_element_type=F32)
-        factor = jnp.where(match, spread, 0.0).astype(BF16)
-        total = total + jnp.dot(factor, returned, preferred_element_type=F32)
-    mixed_ref[...] = total.astype(BF16)
+        factor_ref[term] = jnp.where(match, spread, 0.0).astype(BF16)
+
+
+def join_kernel(map_ref, spread_ref, made_ref, out_ref, sems):
+    replicas, _, width = spread_ref.shape
+    beside = pltpu.make_async_copy(
+        made_ref, out_ref.at[:, :, pl.ds(width, made_ref.shape[2])], sems.at[0]
+    )
+    beside.start()
+
+    def move(old, carry):
+        pltpu.make_async_copy(
+            spread_ref.at[old], out_ref.at[map_ref[old], :, pl.ds(0, width)], sems.at[1]
+        ).start()
+        return carry
+
+    lax.fori_loop(0, replicas, move, 0, unroll=8)
+    beside.wait()
+    pltpu.make_async_copy(spread_ref, out_ref.at[:, :, pl.ds(0, width)], sems.at[1]).wait()
+
+
+def final_kernel(factor_ref, tokens_ref, landed_ref, mixed_ref, gate_ref, up_ref, down_ref, total):
+    step = pl.program_id(0)
+    pieces = landed_ref.shape[0]
+    share = tokens_ref.shape[1]
+    width = landed_ref.shape[2] - share
+    third = width // 3
+    for part, ref in enumerate((gate_ref, up_ref)):
+        ref[...] = landed_ref[:, :, part * third : (part + 1) * third].reshape(ref.shape)
+    blocks = [
+        landed_ref[:, :, 2 * third + k * LANES : 2 * third + (k + 1) * LANES].reshape(
+            pieces, 1, CAP, LANES
+        )
+        for k in range(3)
+    ]
+    down_ref[...] = jnp.concatenate(blocks, axis=1).reshape(down_ref.shape)
+
+    @pl.when(step == 0)
+    def _():
+        total[...] = tokens_ref[...].astype(F32)
+
+    returned = landed_ref[:, :, width:].reshape(pieces * CAP, share)
+    part = jnp.dot(factor_ref[0], returned, preferred_element_type=F32)
+    for term in range(1, factor_ref.shape[0]):
+        part = part + jnp.dot(factor_ref[term], returned, preferred_element_type=F32)
+    total[...] += part
+
+    @pl.when(step == pl.num_programs(0) - 1)
+    def _():
+        mixed_ref[...] = total[...].astype(BF16)
 
 
 def exchange(parts):
@@ -209,13 +222,10 @@
 
     piece_rows = rows // (2 * chips)
     part = jax.ShapeDtypeStruct((chips, piece_rows, 2 * hidden_size), BF16)
-    kept, sent = call(
-        expand_kernel,
-        (part, part),
-        [SMEM, VMEM, VMEM, VMEM],
-        flops=4 * rows * share * hidden_size,
-        moved=8 << 20,
-    )(place, received.reshape(rows, share), gate_local, up_local)
+    expand = call(expand_kernel, part, [SMEM, VMEM, VMEM, VMEM], limit=20)
+    arrived = received.reshape(rows, share)
+    sent = expand((1 - core).reshape(1).astype(I32), arrived, gate_local, up_local)
+    kept = expand(core.reshape(1).astype(I32), arrived, gate_local, up_local)
 
     flip = lambda c: c ^ 1
     mirror = lambda c: chips - 1 - c
@@ -241,20 +251,49 @@
     )
     other = hop(own, lambda c, k: (c, 1 - k))
 
+    routing = (route_ids.T, keep_mask.T, route_gates.T, map_row)
+    made, factors = call(
+        produce_kernel,
+        (
+            jax.ShapeDtypeStruct((replicas, CAP, share), BF16),
+            jax.ShapeDtypeStruct((3, tokens.shape[0], rows), BF16),
+        ),
+        [SMEM] + [VMEM] * 7,
+        limit=20,
+    )(place, own, other, down_local, *routing)
     joined = call(
-        middle_kernel,
+        join_kernel,
         jax.ShapeDtypeStruct((replicas, CAP, width + share), BF16),
-        [SMEM, SMEM, VMEM, VMEM, VMEM, VMEM],
-    )(place, placement_map, spread, own, other, down_local)
+        [SMEM, ANY, ANY],
+        limit=8,
+        out_specs=ANY,
+        scratch_shapes=[pltpu.SemaphoreType.DMA((2,))],
+    )(placement_map, spread, made)
     landed = exchange(joined)
 
+    steps = 4
+    group = tokens.shape[0]
+    half = (share // 2, hidden_size // 2)
     mixed, new_gate, new_up, new_down = call(
         final_kernel,
         tuple(
             jax.ShapeDtypeStruct(a.shape, BF16) for a in (tokens, gate_local, up_local, down_local)
         ),
-        [VMEM] * 6,
-    )(route_ids.T, keep_mask.T, route_gates.T, map_row, tokens, landed)
+        [
+            pl.BlockSpec((3, group, rows // steps), lambda j: (0, 0, j)),
+            pl.BlockSpec((group, share), lambda j: (0, 0)),
+            pl.BlockSpec((replicas // steps, CAP, width + share), lambda j: (j, 0, 0)),
+        ],
+        limit=16,
+        grid=(steps,),
+        out_specs=[
+            pl.BlockSpec((group, share), lambda j: (0, 0)),
+            pl.BlockSpec(half, lambda j: (j % 2, j // 2)),
+            pl.BlockSpec(half, lambda j: (j % 2, j // 2)),
+            pl.BlockSpec((hidden_size, LANES), lambda j: (0, j)),
+        ],
+        scratch_shapes=[pltpu.VMEM((group, share), F32)],
+    )(factors, tokens, landed)
     return (mixed, new_gate[None], new_up[None], new_down[None])
 
 

time: 227 us -> 219 us (0.965)
  the two profiles are of different devices: /device:TPU:7 before, /device:TPU:54 now
where the time goes in v2:
time: 219 us; the launch traced here: 218 us
  blocking collectives  95.9 us (44%)
  waiting for transfers between devices  49.4 us (23%)
  starting transfers between devices  46.7 us (21%)
  Pallas kernels  16.6 us (8%)
  local copies, waits for them, and re-layouts  5.07 us (2%)
  other arithmetic  3.81 us (2%)
    all_to_all x1, blocking collectives, exchange(): lax.all_to_all(parts, 'expert', split_axis=0, concat_axis=0, tiled=True)  95.9 us
    all_to_all x2, waiting for transfers between devices, exchange(): lax.all_to_all(parts, 'expert', split_axis=0, concat_axis=0, tiled=True)  24.8 us
    all_to_all x2, starting transfers between devices, exchange(): lax.all_to_all(parts, 'expert', split_axis=0, concat_axis=0, tiled=True)  24.6 us
    ppermute x9, waiting for transfers between devices, hop(): lax.ppermute(value, 'dp', [(d, 2 * chip + core) for d, (chip, core) in pl...  24.6 us
    ppermute x9, starting transfers between devices, hop(): lax.ppermute(value, 'dp', [(d, 2 * chip + core) for d, (chip, core) in pl...  22.1 us
    unnamed x30, local copies, waits for them, and re-layouts  4.89 us
  transfers between devices with their start and end apart: 11, of which 9 were waited for; matrix products, arithmetic and copies ran while one was open for 2% of the time, Pallas kernels for 3%

profile of v2, /device:TPU:54, one launch (start us, length us, event | category | flops | bytes accessed | tf_op | source)
XLA Modules:
  0.0 218.4 jit_solution(13653773835489113076)
XLA Ops:
  0.6 2.7 %shard_map.112 = bf16[64,16,512]{2,1,0:T(8,128)(2,1)} custom-call(s32[8,128]{1,0:T(8,128)} %bitcast.46, s32[8,128]{1,0:T(8,128)} %bitcast.48, s32[1,64]{1,0:T(1,128)} %bitcast.50, bf16[128,512]{1,0:T(8,128)(2,1)} %tokens_ref.3), custom_call_target="tpu_custom_call" | custom-call | tf_op jit(solution)/shard_map/pallas_call | solution.py:210
  3.3 16.0 %all-to-all-start = ((bf16[64,16,512]{2,1,0:T(8,128)(2,1)}), bf16[64,16,512]{2,1,0:T(8,128)(2,1)S(1)}, u32[]{:S(2)}, u32[]{:S(2)}) async-start(bf16[64,16,512]{2,1,0:T(8,128)(2,1)} %shard_map.112), calls=%async_computation | async-start | bytes 2097152 | tf_op jit(solution)/shard_map/all_to_all | solution.py:185
  19.4 0.0 copy-start
  19.4 0.0 copy-start.2
  19.4 3.4 %shard_map.111 = bf16[64,16,1152]{2,1,0:T(8,128)(2,1)} custom-call(bf16[512,768]{1,0:T(8,128)(2,1)} %bitcast.38, bf16[512,768]{1,0:T(8,128)(2,1)} %bitcast.41, bf16[768,512]{1,0:T(8,128)(2,1)} %bitcast.44), custom_call_target="tpu_custom_call" | custom-call | tf_op jit(solution)/shard_map/pallas_call | solution.py:217
  22.8 24.2 %all-to-all-done = bf16[64,16,512]{2,1,0:T(8,128)(2,1)S(1)} async-done(((bf16[64,16,512]{2,1,0:T(8,128)(2,1)}), bf16[64,16,512]{2,1,0:T(8,128)(2,1)S(1)}, u32[]{:S(2)}, u32[]{:S(2)}) %all-to-all-start) | async-done | bytes 1048608 | tf_op jit(solution)/shard_map/all_to_all | solution.py:185
  47.0 2.2 shard_map.114
  49.2 1.9 collective-permute-start
  51.1 8.6 %all-to-all-start.1 = ((bf16[64,16,1152]{2,1,0:T(8,128)(2,1)}), bf16[64,16,1152]{2,1,0:T(8,128)(2,1)S(1)}, u32[]{:S(2)}, u32[]{:S(2)}) async-start(bf16[64,16,1152]{2,1,0:T(8,128)(2,1)} %shard_map.111), calls=%async_computation.1 | async-start | bytes 4718592 | tf_op jit(solution)/shard_map/all_to_all | solution.py:185
  59.7 1.1 copy-done.1
  60.8 1.1 copy-done.3
  62.0 1.0 shard_map.113
  63.0 1.8 add_convert_fusion
  64.8 0.1 fusion.10
  64.9 0.0 copy-start.12
  65.1 2.4 %collective-permute-start.3 = (bf16[2,128,768]{2,1,0:T(8,128)(2,1)S(1)}, bf16[2,128,768]{2,1,0:T(8,128)(2,1)S(1)}, u32[]{:S(2)}, u32[]{:S(2)}) collective-permute-start(bf16[2,128,768]{2,1,0:T(8,128)(2,1)S(1)} %pad_maximum_fusion.2), channel_id=1, source_target_pairs={{0,6},{1,7},{2,4},{3,5},{4,2},{5,3},{6,0},{7,1},{8,14},{9,15},{10,... | collective-permute-start | bytes 1179656 | tf_op jit(solution)/shard_map/ppermute | solution.py:190
  67.5 2.8 %collective-permute-start.1 = (bf16[2,128,768]{2,1,0:T(8,128)(2,1)S(1)}, bf16[2,128,768]{2,1,0:T(8,128)(2,1)S(1)}, u32[]{:S(2)}, u32[]{:S(2)}) collective-permute-start(bf16[2,128,768]{2,1,0:T(8,128)(2,1)S(1)} %pad_maximum_fusion.1), channel_id=1, source_target_pairs={{0,2},{1,3},{2,0},{3,1},{4,6},{5,7},{6,4},{7,5},{8,10},{9,11},{10,... | collective-permute-start | bytes 1179656 | tf_op jit(solution)/shard_map/ppermute | solution.py:190
  70.3 8.8 %collective-permute-done.3 = bf16[2,128,768]{2,1,0:T(8,128)(2,1)S(1)} collective-permute-done((bf16[2,128,768]{2,1,0:T(8,128)(2,1)S(1)}, bf16[2,128,768]{2,1,0:T(8,128)(2,1)S(1)}, u32[]{:S(2)}, u32[]{:S(2)}) %collective-permute-start.3) | collective-permute-done | bytes 393248 | tf_op jit(solution)/shard_map/ppermute | solution.py:190
  79.1 0.1 convert_element_type.62
  79.2 0.0 copy-start.13
  79.2 0.1 fusion.9
  79.2 0.8 copy-done.13
  80.1 1.9 collective-permute-start.4
  82.0 0.1 convert_element_type.56
  82.1 0.9 copy-done.14
  83.0 2.8 %collective-permute-start.2 = (bf16[128,768]{1,0:T(8,128)(2,1)S(1)}, bf16[128,768]{1,0:T(8,128)(2,1)}, u32[]{:S(2)}, u32[]{:S(2)}) collective-permute-start(bf16[128,768]{1,0:T(8,128)(2,1)S(1)} %fusion.8), channel_id=1, source_target_pairs={{0,6},{1,7},{2,4},{3,5},{4,2},{5,3},{6,0},{7,1},{8,14},{9,15},{10,... | collective-permute-start | bytes 589832 | tf_op jit(solution)/shard_map/ppermute | solution.py:190
  85.8 0.0 copy-start.8
  85.8 0.0 copy-start.9
  85.8 2.1 collective-permute-done.4
  87.9 4.1 %collective-permute-done.2 = bf16[128,768]{1,0:T(8,128)(2,1)} collective-permute-done((bf16[128,768]{1,0:T(8,128)(2,1)S(1)}, bf16[128,768]{1,0:T(8,128)(2,1)}, u32[]{:S(2)}, u32[]{:S(2)}) %collective-permute-start.2) | collective-permute-done | bytes 196640 | tf_op jit(solution)/shard_map/ppermute | solution.py:190
  92.1 1.6 fusion.4
  93.6 2.6 %collective-permute-start.7 = (bf16[128,768]{1,0:T(8,128)(2,1)S(1)}, bf16[128,768]{1,0:T(8,128)(2,1)S(1)}, u32[]{:S(2)}, u32[]{:S(2)}) collective-permute-start(bf16[128,768]{1,0:T(8,128)(2,1)S(1)} %fusion.4), channel_id=1, source_target_pairs={{0,2},{1,3},{2,4},{3,5},{4,6},{5,7},{6,0},{7,1},{8,10},{9,11},{10,... | collective-permute-start | bytes 589832 | tf_op jit(solution)/shard_map/ppermute | solution.py:190
  96.2 3.9 %collective-permute-start.6 = (bf16[128,768]{1,0:T(8,128)(2,1)S(1)}, bf16[128,768]{1,0:T(8,128)(2,1)S(1)}, u32[]{:S(2)}, u32[]{:S(2)}) collective-permute-start(bf16[128,768]{1,0:T(8,128)(2,1)S(1)} %fusion.4), channel_id=1, source_target_pairs={{0,4},{1,5},{2,6},{3,7},{4,0},{5,1},{6,2},{7,3},{8,12},{9,13},{10,... | collective-permute-start | bytes 589832 | tf_op jit(solution)/shard_map/ppermute | solution.py:190
  100.1 1.9 collective-permute-start.5
  102.1 0.6 collective-permute-done.7
  102.6 4.3 %collective-permute-done.6 = bf16[128,768]{1,0:T(8,128)(2,1)S(1)} collective-permute-done((bf16[128,768]{1,0:T(8,128)(2,1)S(1)}, bf16[128,768]{1,0:T(8,128)(2,1)S(1)}, u32[]{:S(2)}, u32[]{:S(2)}) %collective-permute-start.6) | collective-permute-done | bytes 196640 | tf_op jit(solution)/shard_map/ppermute | solution.py:190
  106.9 2.5 %collective-permute-done.5 = bf16[128,768]{1,0:T(8,128)(2,1)S(1)} collective-permute-done((bf16[128,768]{1,0:T(8,128)(2,1)S(1)}, bf16[128,768]{1,0:T(8,128)(2,1)S(1)}, u32[]{:S(2)}, u32[]{:S(2)}) %collective-permute-start.5) | collective-permute-done | bytes 196640 | tf_op jit(solution)/shard_map/ppermute | solution.py:190
  109.4 0.1 pad_maximum_fusion.own_ref
  109.5 1.9 collective-permute-start.8
  111.5 0.1 pad_add_fusion.place_ref
  111.5 2.2 collective-permute-done.8.other_ref
  113.7 2.0 shard_map.115
  115.8 0.9 copy-done.5
  116.7 0.6 all-to-all-done.1.spread_ref
  117.2 2.3 %shard_map.116 = bf16[64,16,1664]{2,1,0:T(8,128)(2,1)S(1)} custom-call(s32[64]{0:T(128)S(1)} %copy-done.10, bf16[64,16,1152]{2,1,0:T(8,128)(2,1)S(1)} %all-to-all-done.1.spread_ref, bf16[64,16,512]{2,1,0:T(8,128)(2,1)S(1)} %get-tuple-element.15.made_ref), custom_call_target="tpu_custom_call" | custom-call | tf_op jit(solution)/shard_map/pallas_call | solution.py:264
  119.6 0.0 copy-start.7
  119.6 95.9 %all_to_all.15.landed_ref = bf16[64,16,1664]{2,1,0:T(8,128)(2,1)S(1)} all-to-all(bf16[64,16,1664]{2,1,0:T(8,128)(2,1)S(1)} %shard_map.116), channel_id=1, replica_groups=mesh['expert'=64,'dp'=8] {'expert'}, dimensions={0} | all-to-all | bytes 6815744 | tf_op jit(solution)/shard_map/all_to_all | solution.py:185
  215.5 2.9 %shard_map.117 = (bf16[128,512]{1,0:T(8,128)(2,1)}, bf16[512,768]{1,0:T(8,128)(2,1)}, bf16[512,768]{1,0:T(8,128)(2,1)}, bf16[768,512]{1,0:T(8,128)(2,1)}) custom-call(bf16[3,128,1024]{2,1,0:T(8,128)(2,1)S(1)} %copy-done.6, bf16[128,512]{1,0:T(8,128)(2,1)S(1)} %copy-done.7, bf16[64,16,1664]{2,1,0:T(8,128)(2,1)S(1)} %all_to_all.15.landed_ref), custom_call_target="tpu_custom_call" | custom-call | tf_op jit(solution)/shard_map/pallas_call | solution.py:277
  (25 shorter events, 0.2 us)
Async XLA Ops:
  3.3 43.7 %all-to-all-start = ((bf16[64,16,512]{2,1,0:T(8,128)(2,1)}), bf16[64,16,512]{2,1,0:T(8,128)(2,1)S(1)}, u32[]{:S(2)}, u32[]{:S(2)}) async-start(bf16[64,16,512]{2,1,0:T(8,128)(2,1)} %shard_map.112), calls=%async_computation | async-start | bytes 2097152 | tf_op jit(solution)/shard_map/all_to_all | solution.py:185
  19.4 27.6 %copy-start = (bf16[1,512,768]{2,1,0:T(8,128)(2,1)S(1)}, bf16[1,512,768]{2,1,0:T(8,128)(2,1)}, u32[]{:S(2)}) copy-start(bf16[1,512,768]{2,1,0:T(8,128)(2,1)} %param.12) | copy-start | bytes 2359300
  19.4 27.6 %copy-start.2 = (bf16[1,512,768]{2,1,0:T(8,128)(2,1)S(1)}, bf16[1,512,768]{2,1,0:T(8,128)(2,1)}, u32[]{:S(2)}) copy-start(bf16[1,512,768]{2,1,0:T(8,128)(2,1)} %param.13) | copy-start | bytes 2359300
  49.2 13.8 %collective-permute-start = (bf16[4,128,1536]{2,1,0:T(8,128)(2,1)}, bf16[4,128,1536]{2,1,0:T(8,128)(2,1)}, u32[]{:S(2)}, u32[]{:S(2)}) collective-permute-start(bf16[4,128,1536]{2,1,0:T(8,128)(2,1)} %shard_map.114), channel_id=1, source_target_pairs={{0,1},{1,0},{2,3},{3,2},{4,5},{5,4},{6,7},{7,6},{8,9},{9,8},{10,11... | collective-permute-start | bytes 4718600 | tf_op jit(solution)/shard_map/ppermute | solution.py:190
  51.1 66.1 %all-to-all-start.1 = ((bf16[64,16,1152]{2,1,0:T(8,128)(2,1)}), bf16[64,16,1152]{2,1,0:T(8,128)(2,1)S(1)}, u32[]{:S(2)}, u32[]{:S(2)}) async-start(bf16[64,16,1152]{2,1,0:T(8,128)(2,1)} %shard_map.111), calls=%async_computation.1 | async-start | bytes 4718592 | tf_op jit(solution)/shard_map/all_to_all | solution.py:185
  59.7 1.1 copy-start.1
  60.8 1.1 copy-start.3
  64.9 14.2 %copy-start.12 = (bf16[4,128,768]{2,1,0:T(8,128)(2,1)}, bf16[4,128,768]{2,1,0:T(8,128)(2,1)S(1)}, u32[]{:S(2)}) copy-start(bf16[4,128,768]{2,1,0:T(8,128)(2,1)S(1)} %get-tuple-element.21) | copy-start | bytes 2359300
  65.1 14.1 %collective-permute-start.3 = (bf16[2,128,768]{2,1,0:T(8,128)(2,1)S(1)}, bf16[2,128,768]{2,1,0:T(8,128)(2,1)S(1)}, u32[]{:S(2)}, u32[]{:S(2)}) collective-permute-start(bf16[2,128,768]{2,1,0:T(8,128)(2,1)S(1)} %pad_maximum_fusion.2), channel_id=1, source_target_pairs={{0,6},{1,7},{2,4},{3,5},{4,2},{5,3},{6,0},{7,1},{8,14},{9,15},{10,... | collective-permute-start | bytes 1179656 | tf_op jit(solution)/shard_map/ppermute | solution.py:190
  67.5 14.4 %collective-permute-start.1 = (bf16[2,128,768]{2,1,0:T(8,128)(2,1)S(1)}, bf16[2,128,768]{2,1,0:T(8,128)(2,1)S(1)}, u32[]{:S(2)}, u32[]{:S(2)}) collective-permute-start(bf16[2,128,768]{2,1,0:T(8,128)(2,1)S(1)} %pad_maximum_fusion.1), channel_id=1, source_target_pairs={{0,2},{1,3},{2,0},{3,1},{4,6},{5,7},{6,4},{7,5},{8,10},{9,11},{10,... | collective-permute-start | bytes 1179656 | tf_op jit(solution)/shard_map/ppermute | solution.py:190
  79.2 0.9 copy-start.13
  80.1 7.9 %collective-permute-start.4 = (bf16[128,768]{1,0:T(8,128)(2,1)S(1)}, bf16[128,768]{1,0:T(8,128)(2,1)}, u32[]{:S(2)}, u32[]{:S(2)}) collective-permute-start(bf16[128,768]{1,0:T(8,128)(2,1)S(1)} %fusion.9), channel_id=1, source_target_pairs={{0,2},{1,3},{2,0},{3,1},{4,6},{5,7},{6,4},{7,5},{8,10},{9,11},{10,... | collective-permute-start | bytes 589832 | tf_op jit(solution)/shard_map/ppermute | solution.py:190
  82.1 0.9 copy-start.14
  83.0 9.1 %collective-permute-start.2 = (bf16[128,768]{1,0:T(8,128)(2,1)S(1)}, bf16[128,768]{1,0:T(8,128)(2,1)}, u32[]{:S(2)}, u32[]{:S(2)}) collective-permute-start(bf16[128,768]{1,0:T(8,128)(2,1)S(1)} %fusion.8), channel_id=1, source_target_pairs={{0,6},{1,7},{2,4},{3,5},{4,2},{5,3},{6,0},{7,1},{8,14},{9,15},{10,... | collective-permute-start | bytes 589832 | tf_op jit(solution)/shard_map/ppermute | solution.py:190
  85.8 27.9 %copy-start.4 = (bf16[1,768,512]{2,1,0:T(8,128)(2,1)S(1)}, bf16[1,768,512]{2,1,0:T(8,128)(2,1)}, u32[]{:S(2)}) copy-start(bf16[1,768,512]{2,1,0:T(8,128)(2,1)} %param.14) | copy-start | bytes 2359300
  85.8 27.9 %copy-start.8 = (s32[128,8]{0,1:T(8,128)S(1)}, s32[128,8]{0,1:T(8,128)}, u32[]{:S(2)}) copy-start(s32[128,8]{0,1:T(8,128)} %param.9) | copy-start | bytes 12292
  85.8 27.9 %copy-start.9 = (s32[128,8]{0,1:T(8,128)S(1)}, s32[128,8]{0,1:T(8,128)}, u32[]{:S(2)}) copy-start(s32[128,8]{0,1:T(8,128)} %param.11) | copy-start | bytes 12292
  85.8 27.9 %copy-start.10 = (s32[64]{0:T(128)S(1)}, s32[64]{0:T(128)}, u32[]{:S(2)}) copy-start(s32[64]{0:T(128)} %map_ref.1) | copy-start | bytes 772
  85.8 27.9 %copy-start.11 = (f32[128,8]{0,1:T(8,128)S(1)}, f32[128,8]{0,1:T(8,128)}, u32[]{:S(2)}) copy-start(f32[128,8]{0,1:T(8,128)} %param.10) | copy-start | bytes 12292
  93.6 9.0 %collective-permute-start.7 = (bf16[128,768]{1,0:T(8,128)(2,1)S(1)}, bf16[128,768]{1,0:T(8,128)(2,1)S(1)}, u32[]{:S(2)}, u32[]{:S(2)}) collective-permute-start(bf16[128,768]{1,0:T(8,128)(2,1)S(1)} %fusion.4), channel_id=1, source_target_pairs={{0,2},{1,3},{2,4},{3,5},{4,6},{5,7},{6,0},{7,1},{8,10},{9,11},{10,... | collective-permute-start | bytes 589832 | tf_op jit(solution)/shard_map/ppermute | solution.py:190
  96.2 10.7 %collective-permute-start.6 = (bf16[128,768]{1,0:T(8,128)(2,1)S(1)}, bf16[128,768]{1,0:T(8,128)(2,1)S(1)}, u32[]{:S(2)}, u32[]{:S(2)}) collective-permute-start(bf16[128,768]{1,0:T(8,128)(2,1)S(1)} %fusion.4), channel_id=1, source_target_pairs={{0,4},{1,5},{2,6},{3,7},{4,0},{5,1},{6,2},{7,3},{8,12},{9,13},{10,... | collective-permute-start | bytes 589832 | tf_op jit(solution)/shard_map/ppermute | solution.py:190
  100.1 9.3 %collective-permute-start.5 = (bf16[128,768]{1,0:T(8,128)(2,1)S(1)}, bf16[128,768]{1,0:T(8,128)(2,1)S(1)}, u32[]{:S(2)}, u32[]{:S(2)}) collective-permute-start(bf16[128,768]{1,0:T(8,128)(2,1)S(1)} %fusion.4), channel_id=1, source_target_pairs={{0,6},{1,7},{2,0},{3,1},{4,2},{5,3},{6,4},{7,5},{8,14},{9,15},{10,... | collective-permute-start | bytes 589832 | tf_op jit(solution)/shard_map/ppermute | solution.py:190
  109.5 4.2 %collective-permute-start.8 = (bf16[4,128,768]{2,1,0:T(8,128)(2,1)S(1)}, bf16[4,128,768]{2,1,0:T(8,128)(2,1)S(1)}, u32[]{:S(2)}, u32[]{:S(2)}) collective-permute-start(bf16[4,128,768]{2,1,0:T(8,128)(2,1)S(1)} %pad_maximum_fusion.own_ref), channel_id=1, source_target_pairs={{0,1},{1,0},{2,3},{3,2},{4,5},{5,4},{6,7},{7,6},{8,9},{9,8},{10,11... | collective-permute-start | bytes 2359304 | tf_op jit(solution)/shard_map/ppermute | solution.py:190
  115.8 0.9 copy-start.5
  119.6 95.9 %copy-start.6 = (bf16[3,128,1024]{2,1,0:T(8,128)(2,1)S(1)}, bf16[3,128,1024]{2,1,0:T(8,128)(2,1)}, u32[]{:S(2)}) copy-start(bf16[3,128,1024]{2,1,0:T(8,128)(2,1)} %copy-done.5) | copy-start | bytes 2359300
  119.6 95.9 %copy-start.7 = (bf16[128,512]{1,0:T(8,128)(2,1)S(1)}, bf16[128,512]{1,0:T(8,128)(2,1)}, u32[]{:S(2)}) copy-start(bf16[128,512]{1,0:T(8,128)(2,1)} %tokens_ref.3) | copy-start | bytes 393220

commit v3 on v2

--- a/solution.py
+++ b/solution.py
@@ -10,6 +10,7 @@
 VMEM = pl.BlockSpec(memory_space=pltpu.VMEM)
 SMEM = pl.BlockSpec(memory_space=pltpu.SMEM)
 ANY = pl.BlockSpec(memory_space=pl.ANY)
+HBM = pl.BlockSpec(memory_space=pltpu.HBM)
 F32, BF16, I32 = jnp.float32, jnp.bfloat16, jnp.int32
 
 
@@ -73,15 +74,21 @@
             out_ref[side * fours : (side + 1) * fours, :, start : start + LANES] = block[:, k]
 
 
-def expand_kernel(place_ref, arrived_ref, gate_ref, up_ref, out_ref):
+def expand_kernel(place_ref, arrived_ref, gate_hbm, up_hbm, out_ref, weights, sems):
     chips, rows = out_ref.shape[:2]
-    hidden = gate_ref.shape[1]
-    for chip in range(chips):
-        start = pl.multiple_of((2 * chip + place_ref[0]) * rows, rows)
-        block = arrived_ref[pl.ds(start, rows), :]
-        for part, weight_ref in enumerate((gate_ref, up_ref)):
+    hidden = weights.shape[2]
+    copies = [
+        pltpu.make_async_copy(ref, weights.at[k], sems.at[k])
+        for k, ref in enumerate((gate_hbm, up_hbm))
+    ]
+    for copy in copies:
+        copy.start()
+    for part, copy in enumerate(copies):
+        copy.wait()
+        for chip in range(chips):
+            start = pl.multiple_of((2 * chip + place_ref[0]) * rows, rows)
             out_ref[chip, :, part * hidden : (part + 1) * hidden] = jnp.dot(
-                block, weight_ref[...], preferred_element_type=F32
+                arrived_ref[pl.ds(start, rows), :], weights[part], preferred_element_type=F32
             ).astype(BF16)
 
 
@@ -222,10 +229,23 @@
 
     piece_rows = rows // (2 * chips)
     part = jax.ShapeDtypeStruct((chips, piece_rows, 2 * hidden_size), BF16)
-    expand = call(expand_kernel, part, [SMEM, VMEM, VMEM, VMEM], limit=20)
+    def expand(first, flops):
+        return call(
+            expand_kernel,
+            part,
+            [SMEM, VMEM, HBM, HBM],
+            limit=20,
+            scratch_shapes=[
+                pltpu.VMEM((2,) + gate_local.shape, BF16),
+                pltpu.SemaphoreType.DMA((2,)),
+            ],
+            cost_estimate=pl.CostEstimate(flops=flops, bytes_accessed=0, transcendentals=0),
+        )(first.reshape(1).astype(I32), arrived, gate_local, up_local)
+
     arrived = received.reshape(rows, share)
-    sent = expand((1 - core).reshape(1).astype(I32), arrived, gate_local, up_local)
-    kept = expand(core.reshape(1).astype(I32), arrived, gate_local, up_local)
+    flops = 2 * rows * share * hidden_size
+    sent = expand(1 - core, flops)
+    kept = expand(core, 64 * flops)
 
     flip = lambda c: c ^ 1
     mirror = lambda c: chips - 1 - c

time: 219 us -> 220 us (level)
  the two profiles are of different devices: /device:TPU:54 before, /device:TPU:48 now
where the time goes in v3:
time: 220 us
  blocking collectives  97.3 us (44%)
  starting transfers between devices  52.7 us (24%)
  waiting for transfers between devices  45.4 us (21%)
  Pallas kernels  15.9 us (7%)
  local copies, waits for them, and re-layouts  5.05 us (2%)
  other arithmetic  2.42 us (1%)
    all_to_all x1, blocking collectives, exchange(): lax.all_to_all(parts, 'expert', split_axis=0, concat_axis=0, tiled=True)  97.3 us
    ppermute x9, starting transfers between devices, hop(): lax.ppermute(value, 'dp', [(d, 2 * chip + core) for d, (chip, core) in pl...  28.1 us
    all_to_all x2, starting transfers between devices, exchange(): lax.all_to_all(parts, 'expert', split_axis=0, concat_axis=0, tiled=True)  24.6 us
    all_to_all x2, waiting for transfers between devices, exchange(): lax.all_to_all(parts, 'expert', split_axis=0, concat_axis=0, tiled=True)  24.3 us
    ppermute x9, waiting for transfers between devices, hop(): lax.ppermute(value, 'dp', [(d, 2 * chip + core) for d, (chip, core) in pl...  21.1 us
    unnamed x26, local copies, waits for them, and re-layouts  4.88 us
  transfers between devices with their start and end apart: 11, of which 9 were waited for; matrix products, arithmetic and copies ran while one was open for 1% of the time, Pallas kernels for 4%

profile of v3, /device:TPU:48, one launch (start us, length us, event | category | flops | bytes accessed | tf_op | source)
XLA Modules:
  0.0 219.7 jit_solution(3565304132013193134)
XLA Ops:
  0.6 2.7 %shard_map.112 = bf16[64,16,512]{2,1,0:T(8,128)(2,1)} custom-call(s32[8,128]{1,0:T(8,128)} %bitcast.46, s32[8,128]{1,0:T(8,128)} %bitcast.48, s32[1,64]{1,0:T(1,128)} %bitcast.50, bf16[128,512]{1,0:T(8,128)(2,1)} %tokens_ref.3), custom_call_target="tpu_custom_call" | custom-call | tf_op jit(solution)/shard_map/pallas_call | solution.py:217
  3.3 16.0 %all-to-all-start = ((bf16[64,16,512]{2,1,0:T(8,128)(2,1)}), bf16[64,16,512]{2,1,0:T(8,128)(2,1)S(1)}, u32[]{:S(2)}, u32[]{:S(2)}) async-start(bf16[64,16,512]{2,1,0:T(8,128)(2,1)} %shard_map.112), calls=%async_computation | async-start | bytes 2097152 | tf_op jit(solution)/shard_map/all_to_all | solution.py:192
  19.4 3.3 %shard_map.111 = bf16[64,16,1152]{2,1,0:T(8,128)(2,1)} custom-call(bf16[512,768]{1,0:T(8,128)(2,1)} %bitcast.38, bf16[512,768]{1,0:T(8,128)(2,1)} %bitcast.41, bf16[768,512]{1,0:T(8,128)(2,1)} %bitcast.44), custom_call_target="tpu_custom_call" | custom-call | tf_op jit(solution)/shard_map/pallas_call | solution.py:224
  22.7 24.3 %all-to-all-done = bf16[64,16,512]{2,1,0:T(8,128)(2,1)S(1)} async-done(((bf16[64,16,512]{2,1,0:T(8,128)(2,1)}), bf16[64,16,512]{2,1,0:T(8,128)(2,1)S(1)}, u32[]{:S(2)}, u32[]{:S(2)}) %all-to-all-start) | async-done | bytes 1048608 | tf_op jit(solution)/shard_map/all_to_all | solution.py:192
  47.0 8.5 %all-to-all-start.1 = ((bf16[64,16,1152]{2,1,0:T(8,128)(2,1)}), bf16[64,16,1152]{2,1,0:T(8,128)(2,1)S(1)}, u32[]{:S(2)}, u32[]{:S(2)}) async-start(bf16[64,16,1152]{2,1,0:T(8,128)(2,1)} %shard_map.111), calls=%async_computation.1 | async-start | bytes 4718592 | tf_op jit(solution)/shard_map/all_to_all | solution.py:192
  55.6 1.1 copy-done
  56.7 1.1 copy-done.1
  57.8 1.3 shard_map.114
  59.1 1.9 collective-permute-start
  61.1 1.3 shard_map.113
  62.4 2.1 collective-permute-done
  64.4 0.4 add_convert_fusion
  64.9 0.1 fusion.10
  65.0 0.0 copy-start.10
  65.1 4.7 %collective-permute-start.3 = (bf16[2,128,768]{2,1,0:T(8,128)(2,1)S(1)}, bf16[2,128,768]{2,1,0:T(8,128)(2,1)S(1)}, u32[]{:S(2)}, u32[]{:S(2)}) collective-permute-start(bf16[2,128,768]{2,1,0:T(8,128)(2,1)S(1)} %pad_maximum_fusion.2), channel_id=1, source_target_pairs={{0,6},{1,7},{2,4},{3,5},{4,2},{5,3},{6,0},{7,1},{8,14},{9,15},{10,... | collective-permute-start | bytes 1179656 | tf_op jit(solution)/shard_map/ppermute | solution.py:197
  69.8 2.1 collective-permute-start.1
  72.0 7.4 %collective-permute-done.3 = bf16[2,128,768]{2,1,0:T(8,128)(2,1)S(1)} collective-permute-done((bf16[2,128,768]{2,1,0:T(8,128)(2,1)S(1)}, bf16[2,128,768]{2,1,0:T(8,128)(2,1)S(1)}, u32[]{:S(2)}, u32[]{:S(2)}) %collective-permute-start.3) | collective-permute-done | bytes 393248 | tf_op jit(solution)/shard_map/ppermute | solution.py:197
  79.3 0.1 convert_element_type.62
  79.4 0.1 fusion.9
  79.5 0.8 copy-done.11
  80.3 2.2 collective-permute-start.4
  82.5 0.1 collective-permute-done.1
  82.6 0.1 convert_element_type.56
  82.7 0.0 copy-start.12
  82.7 0.9 copy-done.12
  83.6 4.3 %collective-permute-start.2 = (bf16[128,768]{1,0:T(8,128)(2,1)S(1)}, bf16[128,768]{1,0:T(8,128)(2,1)}, u32[]{:S(2)}, u32[]{:S(2)}) collective-permute-start(bf16[128,768]{1,0:T(8,128)(2,1)S(1)} %fusion.8), channel_id=1, source_target_pairs={{0,6},{1,7},{2,4},{3,5},{4,2},{5,3},{6,0},{7,1},{8,14},{9,15},{10,... | collective-permute-start | bytes 589832 | tf_op jit(solution)/shard_map/ppermute | solution.py:197
  87.9 0.0 copy-start.2
  87.9 0.0 copy-start.8
  87.9 0.0 copy-start.9
  87.9 0.4 collective-permute-done.4
  88.4 4.2 %collective-permute-done.2 = bf16[128,768]{1,0:T(8,128)(2,1)} collective-permute-done((bf16[128,768]{1,0:T(8,128)(2,1)S(1)}, bf16[128,768]{1,0:T(8,128)(2,1)}, u32[]{:S(2)}, u32[]{:S(2)}) %collective-permute-start.2) | collective-permute-done | bytes 196640 | tf_op jit(solution)/shard_map/ppermute | solution.py:197
  92.6 1.6 fusion.4
  94.2 2.8 %collective-permute-start.7 = (bf16[128,768]{1,0:T(8,128)(2,1)S(1)}, bf16[128,768]{1,0:T(8,128)(2,1)S(1)}, u32[]{:S(2)}, u32[]{:S(2)}) collective-permute-start(bf16[128,768]{1,0:T(8,128)(2,1)S(1)} %fusion.4), channel_id=1, source_target_pairs={{0,2},{1,3},{2,4},{3,5},{4,6},{5,7},{6,0},{7,1},{8,10},{9,11},{10,... | collective-permute-start | bytes 589832 | tf_op jit(solution)/shard_map/ppermute | solution.py:197
  96.9 5.2 %collective-permute-start.6 = (bf16[128,768]{1,0:T(8,128)(2,1)S(1)}, bf16[128,768]{1,0:T(8,128)(2,1)S(1)}, u32[]{:S(2)}, u32[]{:S(2)}) collective-permute-start(bf16[128,768]{1,0:T(8,128)(2,1)S(1)} %fusion.4), channel_id=1, source_target_pairs={{0,4},{1,5},{2,6},{3,7},{4,0},{5,1},{6,2},{7,3},{8,12},{9,13},{10,... | collective-permute-start | bytes 589832 | tf_op jit(solution)/shard_map/ppermute | solution.py:197
  102.1 3.0 %collective-permute-start.5 = (bf16[128,768]{1,0:T(8,128)(2,1)S(1)}, bf16[128,768]{1,0:T(8,128)(2,1)S(1)}, u32[]{:S(2)}, u32[]{:S(2)}) collective-permute-start(bf16[128,768]{1,0:T(8,128)(2,1)S(1)} %fusion.4), channel_id=1, source_target_pairs={{0,6},{1,7},{2,0},{3,1},{4,2},{5,3},{6,4},{7,5},{8,14},{9,15},{10,... | collective-permute-start | bytes 589832 | tf_op jit(solution)/shard_map/ppermute | solution.py:197
  105.2 2.4 %collective-permute-done.6 = bf16[128,768]{1,0:T(8,128)(2,1)S(1)} collective-permute-done((bf16[128,768]{1,0:T(8,128)(2,1)S(1)}, bf16[128,768]{1,0:T(8,128)(2,1)S(1)}, u32[]{:S(2)}, u32[]{:S(2)}) %collective-permute-start.6) | collective-permute-done | bytes 196640 | tf_op jit(solution)/shard_map/ppermute | solution.py:197
  107.6 2.3 %collective-permute-done.5 = bf16[128,768]{1,0:T(8,128)(2,1)S(1)} collective-permute-done((bf16[128,768]{1,0:T(8,128)(2,1)S(1)}, bf16[128,768]{1,0:T(8,128)(2,1)S(1)}, u32[]{:S(2)}, u32[]{:S(2)}) %collective-permute-start.5) | collective-permute-done | bytes 196640 | tf_op jit(solution)/shard_map/ppermute | solution.py:197
  109.9 0.1 pad_maximum_fusion.own_ref
  110.0 1.9 collective-permute-start.8
  111.9 0.1 pad_add_fusion.place_ref
  112.0 2.2 collective-permute-done.8.other_ref
  114.2 2.0 shard_map.115
  116.3 0.0 copy-start.3
  116.3 0.9 copy-done.3
  117.1 2.3 %shard_map.116 = bf16[64,16,1664]{2,1,0:T(8,128)(2,1)S(1)} custom-call(s32[64]{0:T(128)S(1)} %copy-done.8, bf16[64,16,1152]{2,1,0:T(8,128)(2,1)S(1)} %all-to-all-done.1.spread_ref, bf16[64,16,512]{2,1,0:T(8,128)(2,1)S(1)} %get-tuple-element.15.made_ref), custom_call_target="tpu_custom_call" | custom-call | tf_op jit(solution)/shard_map/pallas_call | solution.py:284
  119.5 0.0 copy-start.4
  119.5 97.3 %all_to_all.15.landed_ref = bf16[64,16,1664]{2,1,0:T(8,128)(2,1)S(1)} all-to-all(bf16[64,16,1664]{2,1,0:T(8,128)(2,1)S(1)} %shard_map.116), channel_id=1, replica_groups=mesh['expert'=64,'dp'=8] {'expert'}, dimensions={0} | all-to-all | bytes 6815744 | tf_op jit(solution)/shard_map/all_to_all | solution.py:192
  216.8 2.9 %shard_map.117 = (bf16[128,512]{1,0:T(8,128)(2,1)}, bf16[512,768]{1,0:T(8,128)(2,1)}, bf16[512,768]{1,0:T(8,128)(2,1)}, bf16[768,512]{1,0:T(8,128)(2,1)}) custom-call(bf16[3,128,1024]{2,1,0:T(8,128)(2,1)S(1)} %copy-done.4, bf16[128,512]{1,0:T(8,128)(2,1)S(1)} %copy-done.5, bf16[64,16,1664]{2,1,0:T(8,128)(2,1)S(1)} %all_to_all.15.landed_ref), custom_call_target="tpu_custom_call" | custom-call | tf_op jit(solution)/shard_map/pallas_call | solution.py:297
  (21 shorter events, 0.2 us)
Async XLA Ops:
  3.3 43.7 %all-to-all-start = ((bf16[64,16,512]{2,1,0:T(8,128)(2,1)}), bf16[64,16,512]{2,1,0:T(8,128)(2,1)S(1)}, u32[]{:S(2)}, u32[]{:S(2)}) async-start(bf16[64,16,512]{2,1,0:T(8,128)(2,1)} %shard_map.112), calls=%async_computation | async-start | bytes 2097152 | tf_op jit(solution)/shard_map/all_to_all | solution.py:192
  47.0 70.1 %all-to-all-start.1 = ((bf16[64,16,1152]{2,1,0:T(8,128)(2,1)}), bf16[64,16,1152]{2,1,0:T(8,128)(2,1)S(1)}, u32[]{:S(2)}, u32[]{:S(2)}) async-start(bf16[64,16,1152]{2,1,0:T(8,128)(2,1)} %shard_map.111), calls=%async_computation.1 | async-start | bytes 4718592 | tf_op jit(solution)/shard_map/all_to_all | solution.py:192
  55.6 1.1 copy-start
  56.7 1.1 copy-start.1
  59.1 5.3 %collective-permute-start = (bf16[4,128,1536]{2,1,0:T(8,128)(2,1)S(1)}, bf16[4,128,1536]{2,1,0:T(8,128)(2,1)S(1)}, u32[]{:S(2)}, u32[]{:S(2)}) collective-permute-start(bf16[4,128,1536]{2,1,0:T(8,128)(2,1)S(1)} %shard_map.114), channel_id=1, source_target_pairs={{0,1},{1,0},{2,3},{3,2},{4,5},{5,4},{6,7},{7,6},{8,9},{9,8},{10,11... | collective-permute-start | bytes 4718600 | tf_op jit(solution)/shard_map/ppermute | solution.py:197
  65.0 14.4 %copy-start.10 = (bf16[4,128,768]{2,1,0:T(8,128)(2,1)}, bf16[4,128,768]{2,1,0:T(8,128)(2,1)S(1)}, u32[]{:S(2)}) copy-start(bf16[4,128,768]{2,1,0:T(8,128)(2,1)S(1)} %get-tuple-element.21) | copy-start | bytes 2359300
  65.1 14.3 %collective-permute-start.3 = (bf16[2,128,768]{2,1,0:T(8,128)(2,1)S(1)}, bf16[2,128,768]{2,1,0:T(8,128)(2,1)S(1)}, u32[]{:S(2)}, u32[]{:S(2)}) collective-permute-start(bf16[2,128,768]{2,1,0:T(8,128)(2,1)S(1)} %pad_maximum_fusion.2), channel_id=1, source_target_pairs={{0,6},{1,7},{2,4},{3,5},{4,2},{5,3},{6,0},{7,1},{8,14},{9,15},{10,... | collective-permute-start | bytes 1179656 | tf_op jit(solution)/shard_map/ppermute | solution.py:197
  69.8 12.8 %collective-permute-start.1 = (bf16[2,128,768]{2,1,0:T(8,128)(2,1)S(1)}, bf16[2,128,768]{2,1,0:T(8,128)(2,1)S(1)}, u32[]{:S(2)}, u32[]{:S(2)}) collective-permute-start(bf16[2,128,768]{2,1,0:T(8,128)(2,1)S(1)} %pad_maximum_fusion.1), channel_id=1, source_target_pairs={{0,2},{1,3},{2,0},{3,1},{4,6},{5,7},{6,4},{7,5},{8,10},{9,11},{10,... | collective-permute-start | bytes 1179656 | tf_op jit(solution)/shard_map/ppermute | solution.py:197
  79.4 0.9 copy-start.11
  80.3 8.1 %collective-permute-start.4 = (bf16[128,768]{1,0:T(8,128)(2,1)S(1)}, bf16[128,768]{1,0:T(8,128)(2,1)}, u32[]{:S(2)}, u32[]{:S(2)}) collective-permute-start(bf16[128,768]{1,0:T(8,128)(2,1)S(1)} %fusion.9), channel_id=1, source_target_pairs={{0,2},{1,3},{2,0},{3,1},{4,6},{5,7},{6,4},{7,5},{8,10},{9,11},{10,... | collective-permute-start | bytes 589832 | tf_op jit(solution)/shard_map/ppermute | solution.py:197
  82.7 0.9 copy-start.12
  83.6 9.0 %collective-permute-start.2 = (bf16[128,768]{1,0:T(8,128)(2,1)S(1)}, bf16[128,768]{1,0:T(8,128)(2,1)}, u32[]{:S(2)}, u32[]{:S(2)}) collective-permute-start(bf16[128,768]{1,0:T(8,128)(2,1)S(1)} %fusion.8), channel_id=1, source_target_pairs={{0,6},{1,7},{2,4},{3,5},{4,2},{5,3},{6,0},{7,1},{8,14},{9,15},{10,... | collective-permute-start | bytes 589832 | tf_op jit(solution)/shard_map/ppermute | solution.py:197
  87.9 26.3 %copy-start.2 = (bf16[1,768,512]{2,1,0:T(8,128)(2,1)S(1)}, bf16[1,768,512]{2,1,0:T(8,128)(2,1)}, u32[]{:S(2)}) copy-start(bf16[1,768,512]{2,1,0:T(8,128)(2,1)} %param.14) | copy-start | bytes 2359300
  87.9 26.3 %copy-start.6 = (s32[128,8]{0,1:T(8,128)S(1)}, s32[128,8]{0,1:T(8,128)}, u32[]{:S(2)}) copy-start(s32[128,8]{0,1:T(8,128)} %param.9) | copy-start | bytes 12292
  87.9 26.3 %copy-start.7 = (s32[128,8]{0,1:T(8,128)S(1)}, s32[128,8]{0,1:T(8,128)}, u32[]{:S(2)}) copy-start(s32[128,8]{0,1:T(8,128)} %param.11) | copy-start | bytes 12292
  87.9 26.3 %copy-start.8 = (s32[64]{0:T(128)S(1)}, s32[64]{0:T(128)}, u32[]{:S(2)}) copy-start(s32[64]{0:T(128)} %map_ref.1) | copy-start | bytes 772
  87.9 26.3 %copy-start.9 = (f32[128,8]{0,1:T(8,128)S(1)}, f32[128,8]{0,1:T(8,128)}, u32[]{:S(2)}) copy-start(f32[128,8]{0,1:T(8,128)} %param.10) | copy-start | bytes 12292
  94.2 11.0 %collective-permute-start.7 = (bf16[128,768]{1,0:T(8,128)(2,1)S(1)}, bf16[128,768]{1,0:T(8,128)(2,1)S(1)}, u32[]{:S(2)}, u32[]{:S(2)}) collective-permute-start(bf16[128,768]{1,0:T(8,128)(2,1)S(1)} %fusion.4), channel_id=1, source_target_pairs={{0,2},{1,3},{2,4},{3,5},{4,6},{5,7},{6,0},{7,1},{8,10},{9,11},{10,... | collective-permute-start | bytes 589832 | tf_op jit(solution)/shard_map/ppermute | solution.py:197
  96.9 10.6 %collective-permute-start.6 = (bf16[128,768]{1,0:T(8,128)(2,1)S(1)}, bf16[128,768]{1,0:T(8,128)(2,1)S(1)}, u32[]{:S(2)}, u32[]{:S(2)}) collective-permute-start(bf16[128,768]{1,0:T(8,128)(2,1)S(1)} %fusion.4), channel_id=1, source_target_pairs={{0,4},{1,5},{2,6},{3,7},{4,0},{5,1},{6,2},{7,3},{8,12},{9,13},{10,... | collective-permute-start | bytes 589832 | tf_op jit(solution)/shard_map/ppermute | solution.py:197
  102.1 7.8 %collective-permute-start.5 = (bf16[128,768]{1,0:T(8,128)(2,1)S(1)}, bf16[128,768]{1,0:T(8,128)(2,1)S(1)}, u32[]{:S(2)}, u32[]{:S(2)}) collective-permute-start(bf16[128,768]{1,0:T(8,128)(2,1)S(1)} %fusion.4), channel_id=1, source_target_pairs={{0,6},{1,7},{2,0},{3,1},{4,2},{5,3},{6,4},{7,5},{8,14},{9,15},{10,... | collective-permute-start | bytes 589832 | tf_op jit(solution)/shard_map/ppermute | solution.py:197
  110.0 4.2 %collective-permute-start.8 = (bf16[4,128,768]{2,1,0:T(8,128)(2,1)S(1)}, bf16[4,128,768]{2,1,0:T(8,128)(2,1)S(1)}, u32[]{:S(2)}, u32[]{:S(2)}) collective-permute-start(bf16[4,128,768]{2,1,0:T(8,128)(2,1)S(1)} %pad_maximum_fusion.own_ref), channel_id=1, source_target_pairs={{0,1},{1,0},{2,3},{3,2},{4,5},{5,4},{6,7},{7,6},{8,9},{9,8},{10,11... | collective-permute-start | bytes 2359304 | tf_op jit(solution)/shard_map/ppermute | solution.py:197
  116.3 0.9 copy-start.3
  119.5 97.3 %copy-start.4 = (bf16[3,128,1024]{2,1,0:T(8,128)(2,1)S(1)}, bf16[3,128,1024]{2,1,0:T(8,128)(2,1)}, u32[]{:S(2)}) copy-start(bf16[3,128,1024]{2,1,0:T(8,128)(2,1)} %copy-done.3) | copy-start | bytes 2359300
  119.5 97.3 %copy-start.5 = (bf16[128,512]{1,0:T(8,128)(2,1)S(1)}, bf16[128,512]{1,0:T(8,128)(2,1)}, u32[]{:S(2)}) copy-start(bf16[128,512]{1,0:T(8,128)(2,1)} %tokens_ref.3) | copy-start | bytes 393220
